TPU v7x, 32 devices: a whole 2x2x4 slice. The times are simulated.
32 devices in a mesh: dp: 8 (over z, x), mp: 4 (over y, core).
Axes of the slice: x: 2, y: 2, z: 4, core: 2. Of those that a mesh axis runs over, the one named last changes fastest.
Arguments:
- words: bfloat16 [16, 512, 768], P('dp'), may hold values from -6 to 6
- word_extra: int32 [16], P('dp'), may hold values from 1 to 448, 4096 in all
- span_pos: int32 [16, 128], P('dp'), may hold values from 0 to 511
- span_len: int32 [16, 128], P('dp'), may hold values from 1 to 4
- entity_shard: int32 [16, 128, 1], P('dp'), may hold values from 0 to 7; in each aligned block of 256 rows (0 to 255, 256 to 511, ..., all dimensions but the last counted through in order) at most 64 rows name the same one
- entity_row: int32 [16, 128], P('dp'), may hold values from 0 to 7999
- targets: int32 [16, 16], replicated, may hold values from 0 to 63999, as said below
- table: bfloat16 [64000, 256], P('dp', 'mp'), may hold values from -1.125 to 1.125
- ent_proj: bfloat16 [256, 768], P('mp'), may hold values from -2 to 2
- query_weight: bfloat16 [4, 768, 768], P(None, None, 'mp'), may hold values from -0.21875 to 0.21875
- w_key: bfloat16 [768, 768], P(None, 'mp'), may hold values from -0.21875 to 0.21875
- w_value: bfloat16 [768, 768], P(None, 'mp'), may hold values from -0.21875 to 0.21875
- w_out: bfloat16 [768, 768], P('mp'), may hold values from -1.25 to 1.25
- gain_attn: float32 [768], replicated, may hold values from 0.5 to 1.5
- bias_attn: float32 [768], replicated, may hold values from -3 to 3
- w_up: bfloat16 [768, 3072], P(None, 'mp'), may hold values from -0.21875 to 0.21875
- w_down: bfloat16 [3072, 768], P('mp'), may hold values from -0.109375 to 0.109375
- gain_ffn: float32 [768], replicated, may hold values from 0.5 to 1.5
- bias_ffn: float32 [768], replicated, may hold values from -3 to 3
- w_head: bfloat16 [768, 256], replicated, may hold values from -0.21875 to 0.21875
- gain_head: float32 [256], replicated, may hold values from 0.5 to 1.5
- cot_words: bfloat16 [16, 512, 768], P('dp'), may hold values from -6 to 6
- cot_ents: bfloat16 [16, 128, 768], P('dp'), may hold values from -6 to 6
Outputs:
- out_words: bfloat16 [16, 512, 768], P('dp')
- out_ents: bfloat16 [16, 128, 768], P('dp')
- loss: float32 [256], replicated
- grad_words: float32 [16, 512, 768], P('dp')
- grad_table: float32 [64000, 256], P('dp', 'mp')
- grad_ent_proj: float32 [256, 768], P('mp')
- grad_query: float32 [4, 768, 768], P(None, None, 'mp')
- grad_key: float32 [768, 768], P(None, 'mp')
- grad_value: float32 [768, 768], P(None, 'mp')
- grad_out: float32 [768, 768], P('mp')
- grad_gain_attn: float32 [768], replicated
- grad_bias_attn: float32 [768], replicated
- grad_up: float32 [768, 3072], P(None, 'mp')
- grad_down: float32 [3072, 768], P('mp')
- grad_gain_ffn: float32 [768], replicated
- grad_bias_ffn: float32 [768], replicated
- grad_head: float32 [768, 256], replicated
- grad_gain_head: float32 [256], replicated
Inputs may be any that keep to these rules, and one draw needn't show every extreme that they name: `entity_shard`: among the entity slots of one index of dp, at most 64 name the same table shard; in some of those blocks one shard is named exactly 64 times. `word_extra`: some sequence holds all 512 words. Each table shard of 8000 rows holds the targets of exactly 32 scored slots.
All inputs are finite; a program needn't handle non-finite values. No bound on the sum of `word_extra` on one device may be relied on, other than what follows from the above.
Results may differ from a plain program's by a relative error of at most 0.017.
Values may be sent and summed in bfloat16 or wider, within the bound.
A program may use at most 192 MiB of HBM per device.

v0:
```python
import math

import jax
import jax.numpy as jnp
from jax import lax
from jax.sharding import PartitionSpec as P

DH = 64
SPANW = 4


EPSILON = 1e-05
MASKED_SCORE = -1000000000.0


def combined_all(part, axis, combine):
    gathered = jax.tree.map(lambda a: lax.all_gather(a, axis), part)

    def take(source):
        return jax.tree.map(lambda a: lax.dynamic_index_in_dim(a, source, 0, False), gathered)

    return lax.fori_loop(
        1, lax.axis_size(axis), lambda source, state: combine(state, take(source)), take(0)
    )


def matmul(first_op, second_op):
    return jnp.dot(first_op, second_op, preferred_element_type=jnp.float32)


def contract_product(form, first_op, second_op):
    return jnp.einsum(form, first_op, second_op, preferred_element_type=jnp.float32)


def normalize(source, gain_vec, shift_vec):
    center = source - jnp.mean(source, axis=-1, keepdims=True)
    inv_scale = lax.rsqrt(jnp.mean(center * center, axis=-1, keepdims=True) + EPSILON)
    return center * inv_scale * gain_vec + shift_vec


def gelu_exact(source):
    return jax.nn.gelu(source, approximate=False)


def head_map(head_pre, gain_vec):
    return normalize(gelu_exact(head_pre), gain_vec, 0.0)


def combine(first_set, second_set):
    new_top = jnp.maximum(first_set[0], second_set[0])
    new_total = first_set[1] * jnp.exp(first_set[0] - new_top) + second_set[1] * jnp.exp(
        second_set[0] - new_top
    )
    return (new_top, new_total, first_set[2] + second_set[2])


def shards(
    words,
    word_extra,
    span_pos,
    span_len,
    entity_shard,
    entity_row,
    targets,
    table,
    ent_proj,
    query_weight,
    w_key,
    w_value,
    w_out,
    gain_attn,
    bias_attn,
    w_up,
    w_down,
    gain_ffn,
    bias_ffn,
    w_head,
    gain_head,
    cot_words,
    cot_ents,
):
    n_dp = lax.axis_size("dp")
    seq_count, word_length, model_width = words.shape
    ent_len = span_pos.shape[1]
    masked_len = targets.shape[1]
    tokens_len = word_length + ent_len
    rows_dev, cols_dev = table.shape
    local_width = w_key.shape[1]
    heads_local = local_width // DH
    ent_total = seq_count * ent_len
    owners = entity_shard.reshape(ent_total)
    wanted = entity_row.reshape(ent_total)
    capacity = max(2, 2 * ent_total // n_dp)
    owner_onehot = (owners[:, None] == jnp.arange(n_dp, dtype=jnp.int32)[None, :]).astype(
        jnp.float32
    )
    order_index = jnp.arange(ent_total, dtype=jnp.int32)
    earlier = (order_index[:, None] > order_index[None, :]).astype(jnp.float32)
    before = matmul(earlier, owner_onehot)
    slot_rank = jnp.sum(before * owner_onehot, axis=1).astype(jnp.int32)
    requests = jnp.full((n_dp, capacity), -1, jnp.int32).at[owners, slot_rank].set(wanted)
    received = lax.all_to_all(requests, "dp", split_axis=0, concat_axis=0, tiled=True)
    present = received >= 0
    picked = jnp.take(table, jnp.maximum(received, 0), axis=0)
    picked = jnp.where(present[..., None], picked, jnp.zeros_like(picked))
    back_rows = lax.all_to_all(picked, "dp", split_axis=0, concat_axis=0, tiled=True)
    vec_cols = back_rows[owners, slot_rank]
    ent_vectors = lax.psum(matmul(vec_cols, ent_proj), "mp")
    word_count = word_length // 8 + word_extra
    span_start = span_pos * (word_count[:, None] - SPANW) // word_length
    positions = jnp.arange(word_length, dtype=jnp.int32)
    inside = (positions[None, None, :] >= span_start[..., None]) & (
        positions[None, None, :] < (span_start + span_len)[..., None]
    )
    span_total = contract_product("sep,spd->sed", inside.astype(jnp.bfloat16), words)
    span_width = span_len.astype(jnp.float32)[..., None]
    ent_low = (
        ent_vectors.reshape(seq_count, ent_len, model_width) + span_total / span_width
    ).astype(jnp.bfloat16)
    stream = jnp.concatenate([words, ent_low], axis=1)
    word_query = contract_product("rpa,gay->grpy", words, query_weight[:2])
    q_ent = contract_product("sed,kdh->kseh", ent_low, query_weight[2:])
    to_words = jnp.concatenate([word_query[0], q_ent[0]], axis=1).astype(jnp.bfloat16)
    to_ents = jnp.concatenate([word_query[1], q_ent[1]], axis=1).astype(jnp.bfloat16)
    key_rows = contract_product("snd,dh->snh", stream, w_key).astype(jnp.bfloat16)
    value_rows = contract_product("snd,dh->snh", stream, w_value).astype(jnp.bfloat16)
    head_shape = (seq_count, tokens_len, heads_local, DH)
    words_heads = to_words.reshape(head_shape)
    ents_heads = to_ents.reshape(head_shape)
    keys_heads = key_rows.reshape(head_shape)
    values_heads = value_rows.reshape(head_shape)
    key_valid = jnp.concatenate(
        [positions[None, :] < word_count[:, None], jnp.ones((seq_count, ent_len), dtype=bool)],
        axis=1,
    )

    def score_rows():
        word_part = contract_product("sqhc,skhc->shqk", words_heads, keys_heads[:, :word_length])
        ent_part = contract_product("sqhc,skhc->shqk", ents_heads, keys_heads[:, word_length:])
        raw_scores = jnp.concatenate([word_part, ent_part], axis=-1) * 0.125
        return jnp.where(key_valid[:, None, None, :], raw_scores, MASKED_SCORE)

    scores = score_rows()
    row_max = jnp.max(scores, axis=-1, keepdims=True)
    log_total = row_max + jnp.log(jnp.sum(jnp.exp(scores - row_max), axis=-1, keepdims=True))
    prob_low = jnp.exp(scores - log_total).astype(jnp.bfloat16)
    context = (
        contract_product("shqk,skhc->sqhc", prob_low, values_heads)
        .reshape(seq_count * tokens_len, local_width)
        .astype(jnp.bfloat16)
    )
    attn_sum = lax.psum(matmul(context, w_out), "mp")
    pre_first = stream.reshape(seq_count * tokens_len, model_width).astype(jnp.float32) + attn_sum
    first_norm, first_back = jax.vjp(normalize, pre_first, gain_attn, bias_attn)
    first_low = first_norm.astype(jnp.bfloat16)
    pre_act = matmul(first_low, w_up)
    hidden_f, gelu_back = jax.vjp(gelu_exact, pre_act)
    hidden = hidden_f.astype(jnp.bfloat16)
    ffn_sum = lax.psum(matmul(hidden, w_down), "mp")
    pre_second = first_norm + ffn_sum
    output, second_back = jax.vjp(normalize, pre_second, gain_ffn, bias_ffn)
    out_low = output.astype(jnp.bfloat16).reshape(seq_count, tokens_len, model_width)
    out_words = out_low[:, :word_length]
    out_ents = out_low[:, word_length:]
    head_in = out_low[:, word_length : word_length + masked_len].reshape(
        seq_count * masked_len, model_width
    )
    head_pre = matmul(head_in, w_head)
    head_vec, head_back = jax.vjp(head_map, head_pre, gain_head)
    all_head = lax.all_gather(head_vec.astype(jnp.bfloat16), "dp", axis=0, tiled=True)
    table_full = lax.all_gather(table, "mp", axis=1, tiled=True)
    masked_total = all_head.shape[0]
    ent_width = table_full.shape[1]
    row_offset = lax.axis_index("dp") * rows_dev
    local_target = targets.reshape(-1) - row_offset
    is_mine = (local_target >= 0) & (local_target < rows_dev)
    target_index = jnp.clip(local_target, 0, rows_dev - 1)
    target_rows = jnp.take(table_full, target_index, axis=0)
    target_logit = jnp.where(
        is_mine,
        jnp.sum(all_head.astype(jnp.float32) * target_rows.astype(jnp.float32), axis=-1),
        0.0,
    )
    block_rows = math.gcd(masked_total, 256)
    block_count = masked_total // block_rows
    head_blocks = all_head.reshape(block_count, block_rows, ent_width)

    def logits_of(head_block):
        return contract_product("md,rd->mr", head_block, table_full)

    def block_stats(head_block):
        logits = logits_of(head_block)
        row_top = jnp.max(logits, axis=1)
        return (row_top, jnp.sum(jnp.exp(logits - row_top[:, None]), axis=1))

    block_top, block_total = lax.map(block_stats, head_blocks)
    global_top, global_total, global_target = combined_all(
        (block_top.reshape(masked_total), block_total.reshape(masked_total), target_logit),
        "dp",
        combine,
    )
    head_total = global_top + jnp.log(global_total)
    loss = head_total - global_target
    my_cols = lax.dynamic_slice_in_dim(all_head, lax.axis_index("mp") * cols_dev, cols_dev, 1)

    def block_back(running, inputs):
        head_block, col_block, total_block = inputs
        weight_low = jnp.exp(logits_of(head_block) - total_block[:, None]).astype(jnp.bfloat16)
        grad_block = matmul(weight_low, table_full)
        running = running + contract_product("mr,mc->rc", weight_low, col_block)
        return (running, grad_block)

    table_grad, grad_head_vec = lax.scan(
        block_back,
        jnp.zeros((rows_dev, cols_dev), jnp.float32),
        (
            head_blocks,
            my_cols.reshape(block_count, block_rows, cols_dev),
            head_total.reshape(block_count, block_rows),
        ),
    )
    grad_head_vec = grad_head_vec.reshape(masked_total, ent_width) - jnp.where(
        is_mine[:, None], target_rows.astype(jnp.float32), 0.0
    )
    table_grad = table_grad.at[target_index].add(
        -jnp.where(is_mine[:, None], my_cols.astype(jnp.float32), 0.0)
    )
    grad_head_mine = lax.psum_scatter(grad_head_vec, "dp", scatter_dimension=0, tiled=True)
    d_head_pre, grad_gain_head = head_back(grad_head_mine)
    d_head_low = d_head_pre.astype(jnp.bfloat16)
    grad_head = contract_product("md,me->de", head_in, d_head_low)
    d_head_in = contract_product("me,de->md", d_head_low, w_head)
    d_output = jnp.concatenate([cot_words, cot_ents], axis=1).astype(jnp.float32)
    d_output = d_output.at[:, word_length : word_length + masked_len].add(
        d_head_in.reshape(seq_count, masked_len, model_width)
    )
    d_output = d_output.reshape(seq_count * tokens_len, model_width)
    d_second, grad_gain_ffn, grad_bias_ffn = second_back(d_output)
    d_ffn = d_second.astype(jnp.bfloat16)
    grad_down = contract_product("tf,td->fd", hidden, d_ffn)
    d_hidden = contract_product("td,fd->tf", d_ffn, w_down)
    d_pre_act = gelu_back(d_hidden)[0].astype(jnp.bfloat16)
    grad_up = contract_product("td,tf->df", first_low, d_pre_act)
    d_first = d_second + lax.psum(contract_product("tf,df->td", d_pre_act, w_up), "mp")
    d_pre_first, grad_gain_attn, grad_bias_attn = first_back(d_first)
    d_attn = d_pre_first.astype(jnp.bfloat16)
    grad_out = contract_product("th,td->hd", context, d_attn)
    d_context = (
        contract_product("td,hd->th", d_attn, w_out).astype(jnp.bfloat16).reshape(head_shape)
    )
    prob_rows = jnp.exp(score_rows() - log_total)
    prob_again = prob_rows.astype(jnp.bfloat16)
    d_probs = contract_product("sqhc,skhc->shqk", d_context, values_heads)
    d_values = (
        contract_product("shqk,sqhc->skhc", prob_again, d_context)
        .astype(jnp.bfloat16)
        .reshape(seq_count, tokens_len, local_width)
    )
    d_scores = (
        prob_rows * (d_probs - jnp.sum(prob_rows * d_probs, axis=-1, keepdims=True))
    ).astype(jnp.bfloat16)
    word_bound_gradient = (
        (
            contract_product(
                "shqk,skhc->sqhc", d_scores[..., :word_length], keys_heads[:, :word_length]
            )
            * 0.125
        )
        .astype(jnp.bfloat16)
        .reshape(seq_count, tokens_len, local_width)
    )
    entity_bound_gradient = (
        (
            contract_product(
                "shqk,skhc->sqhc", d_scores[..., word_length:], keys_heads[:, word_length:]
            )
            * 0.125
        )
        .astype(jnp.bfloat16)
        .reshape(seq_count, tokens_len, local_width)
    )
    d_keys_words = (
        contract_product("shqk,sqhc->skhc", d_scores[..., :word_length], words_heads) * 0.125
    )
    d_keys_ents = (
        contract_product("shqk,sqhc->skhc", d_scores[..., word_length:], ents_heads) * 0.125
    )
    d_keys = (
        jnp.concatenate([d_keys_words, d_keys_ents], axis=1)
        .astype(jnp.bfloat16)
        .reshape(seq_count, tokens_len, local_width)
    )
    grad_query = jnp.stack(
        [
            contract_product("yir,yiq->rq", words, word_bound_gradient[:, :word_length]),
            contract_product("yir,yiq->rq", words, entity_bound_gradient[:, :word_length]),
            contract_product("sed,seh->dh", ent_low, word_bound_gradient[:, word_length:]),
            contract_product("sed,seh->dh", ent_low, entity_bound_gradient[:, word_length:]),
        ]
    )
    grad_key = contract_product("snd,snh->dh", stream, d_keys)
    grad_value = contract_product("snd,snh->dh", stream, d_values)
    word_stream_gradient = contract_product(
        "vcr,er->vce", word_bound_gradient[:, :word_length], query_weight[0]
    ) + contract_product("vcr,er->vce", entity_bound_gradient[:, :word_length], query_weight[1])
    d_stream_ent = contract_product(
        "seh,dh->sed", word_bound_gradient[:, word_length:], query_weight[2]
    ) + contract_product("seh,dh->sed", entity_bound_gradient[:, word_length:], query_weight[3])
    d_stream = (
        jnp.concatenate([word_stream_gradient, d_stream_ent], axis=1)
        + contract_product("snh,dh->snd", d_keys, w_key)
        + contract_product("snh,dh->snd", d_values, w_value)
    )
    d_stream_sum = lax.psum(d_stream, "mp")
    d_total = d_pre_first.reshape(seq_count, tokens_len, model_width) + d_stream_sum
    d_ent = d_total[:, word_length:].astype(jnp.bfloat16)
    grad_words = d_total[:, :word_length] + jnp.einsum(
        "sep,sed->spd",
        inside.astype(jnp.float32),
        d_ent.astype(jnp.float32) / span_width,
        precision=lax.Precision.HIGHEST,
    )
    d_ent_flat = d_ent.reshape(ent_total, model_width)
    grad_ent_proj = contract_product("tc,td->cd", vec_cols, d_ent_flat)
    d_vec = contract_product("td,cd->tc", d_ent_flat, ent_proj).astype(jnp.bfloat16)
    outbox = jnp.zeros((n_dp, capacity, cols_dev), jnp.bfloat16).at[owners, slot_rank].set(d_vec)
    inbox = lax.all_to_all(outbox, "dp", split_axis=0, concat_axis=0, tiled=True)
    table_grad = table_grad.at[jnp.maximum(received, 0)].add(
        jnp.where((received >= 0)[..., None], inbox.astype(jnp.float32), 0.0)
    )
    (
        grad_query,
        grad_key,
        grad_value,
        grad_out,
        grad_gain_attn,
        grad_bias_attn,
        grad_ent_proj,
        grad_up,
        grad_down,
        grad_gain_ffn,
        grad_bias_ffn,
        grad_head,
        grad_gain_head,
    ) = lax.psum(
        (
            grad_query,
            grad_key,
            grad_value,
            grad_out,
            grad_gain_attn,
            grad_bias_attn,
            grad_ent_proj,
            grad_up,
            grad_down,
            grad_gain_ffn,
            grad_bias_ffn,
            grad_head,
            grad_gain_head,
        ),
        "dp",
    )
    return (
        out_words,
        out_ents,
        loss,
        grad_words,
        table_grad,
        grad_ent_proj,
        grad_query,
        grad_key,
        grad_value,
        grad_out,
        grad_gain_attn,
        grad_bias_attn,
        grad_up,
        grad_down,
        grad_gain_ffn,
        grad_bias_ffn,
        grad_head,
        grad_gain_head,
    )


def solution(mesh):
    return jax.shard_map(
        shards,
        mesh=mesh,
        in_specs=(
            P("dp", None, None),
            P("dp"),
            P("dp", None),
            P("dp", None),
            P("dp", None, None),
            P("dp", None),
            P(),
            P("dp", "mp"),
            P("mp", None),
            P(None, None, "mp"),
            P(None, "mp"),
            P(None, "mp"),
            P("mp", None),
            P(),
            P(),
            P(None, "mp"),
            P("mp", None),
            P(),
            P(),
            P(),
            P(),
            P("dp", None, None),
            P("dp", None, None),
        ),
        out_specs=(
            P("dp", None, None),
            P("dp", None, None),
            P(),
            P("dp", None, None),
            P("dp", "mp"),
            P("mp", None),
            P(None, None, "mp"),
            P(None, "mp"),
            P(None, "mp"),
            P("mp", None),
            P(),
            P(),
            P(None, "mp"),
            P("mp", None),
            P(),
            P(),
            P(),
            P(),
        ),
        check_vma=False,
    )
```

profile of v0, /device:TPU:0, one launch (start us, length us, event | category | flops | bytes accessed | tf_op | source)
XLA Modules:
  0.0 1103.9 jit_solution(9905556814473912743)
XLA Ops:
  9.5 38.7 %scatter_fusion = s32[8,64]{1,0:T(8,128)} fusion(s32[8,64]{1,0:T(8,128)} %broadcast_in_dim.161, s32[256]{0:T(256)S(1)} %bitcast.215, s32[256]{0:T(256)} %bitcast.276), kind=kCustom, calls=%fused_computation.3 | custom fusion | bytes 5120 | tf_op jit(solution)/shard_map/scatter | solution.py:101
  48.2 7.3 all-to-all-start
  71.8 6.8 all-to-all-done.1
  83.9 30.0 %all-reduce.10.cloned.1.call-done = f32[2,128,768]{2,1,0:T(8,128)} async-done(((f32[2,128,768]{2,1,0:T(8,128)}), f32[2,128,768]{2,1,0:T(8,128)}) %all-reduce.10.cloned.1.call-update) | async-done | bytes 786448 | tf_op jit(solution)/shard_map/psum | solution.py:108
  135.2 78.4 %all-reduce.12.cloned.1.call-done = f32[1280,768]{1,0:T(8,128)} async-done(((f32[1280,768]{1,0:T(8,128)}), f32[1280,768]{1,0:T(8,128)}) %all-reduce.12.cloned.1.call-update) | async-done | bytes 3932176 | tf_op jit(solution)/shard_map/psum | solution.py:152
  219.3 11.0 multiply_convert_fusion.1
  246.8 69.9 %all-reduce.14.cloned.1.call-done = f32[1280,768]{1,0:T(8,128)} async-done(((f32[1280,768]{1,0:T(8,128)}), f32[1280,768]{1,0:T(8,128)}) %all-reduce.14.cloned.1.call-update) | async-done | bytes 3932176 | tf_op jit(solution)/shard_map/psum | solution.py:159
  326.3 32.6 %all_gather.16 = bf16[256,256]{1,0:T(8,128)(2,1)} all-gather(bf16[32,256]{1,0:T(8,128)(2,1)S(1)} %multiply_convert_fusion.2), channel_id=1, replica_groups=mesh['dp'=8,'mp'=4] {'dp'}, dimensions={0}, use_global_device_ids=true | all-gather | bytes 147456 | tf_op jit(solution)/shard_map/all_gather | solution.py:170
  366.1 20.4 %all-gather.3 = f32[8,1,256]{2,1,0:T(1,128)S(1)} all-gather(f32[1,1,256]{2,1,0:T(1,128)S(1)} %bitcast.272), channel_id=3, replica_groups=mesh['dp'=8,'mp'=4] {'dp'}, dimensions={0}, use_global_device_ids=true | all-gather | bytes 9216 | tf_op jit(solution)/shard_map/all_gather | solution.py:17
  387.7 16.7 %all-gather.2 = f32[8,1,256]{2,1,0:T(1,128)S(1)} all-gather(f32[1,1,256]{2,1,0:T(1,128)S(1)} %bitcast.270), channel_id=2, replica_groups=mesh['dp'=8,'mp'=4] {'dp'}, dimensions={0}, use_global_device_ids=true | all-gather | bytes 9216 | tf_op jit(solution)/shard_map/all_gather | solution.py:17
  405.5 6.4 copy.91
  418.2 18.3 %all-gather.4 = f32[8,1,256]{2,1,0:T(1,128)S(1)} all-gather(f32[1,1,256]{2,1,0:T(1,128)S(1)} %select_bitcast_fusion), channel_id=1, replica_groups=mesh['dp'=8,'mp'=4] {'dp'}, dimensions={0}, use_global_device_ids=true | all-gather | bytes 9216 | tf_op jit(solution)/shard_map/all_gather | solution.py:17
  437.6 27.5 %while.13 = (s32[]{:T(128)}, f32[256]{0:T(256)}, f32[256]{0:T(256)}, f32[256]{0:T(256)}, f32[8,256]{1,0:T(8,128)}, /*index=5*/f32[8,256]{1,0:T(8,128)}, f32[8,256]{1,0:T(8,128)}, s32[]{:T(128)}, s32[]{:T(128)}, s32[]{:T(128)}) while((s32[]{:T(128)}, f32[256]{0:T(256)}, f32[256]{0:T(256)}, f32[256]{0:T(256)}, f32[8,256]{1,0:T(8,128)}, ...), condition=%wide.region_17.18_spmd, body=%wide.region_16.17_spmd.sunk | while | flops 1797 | bytes 15511 | solution.py:22
  467.0 6.7 convolution_subtract_fusion
  477.6 54.1 %reduce-scatter.2.cloned.1.call-done = f32[32,256]{1,0:T(8,128)} async-done(((f32[256,256]{1,0:T(8,128)}), f32[32,256]{1,0:T(8,128)}) %reduce-scatter.2.cloned.1.call-update) | async-done | bytes 32784 | tf_op jit(solution)/shard_map/reduce_scatter | solution.py:228
  566.0 71.5 %all-reduce.16.cloned.1.call-done = f32[1280,768]{1,0:T(8,128)} async-done(((f32[1280,768]{1,0:T(8,128)}), f32[1280,768]{1,0:T(8,128)}) %all-reduce.16.cloned.1.call-update) | async-done | bytes 3932176 | tf_op jit(solution)/shard_map/psum | solution.py:244
  649.5 13.6 %multiply_convert_fusion = bf16[2,3,640,640]{2,3,1,0:T(8,128)(2,1)} fusion(f32[2,3,640]{2,1,0:T(4,128)S(1)} %copy-done.87, bf16[2,640,3,64]{1,3,2,0:T(8,128)(2,1)} %bitcast.279, bf16[2,640,3,64]{1,0,3,2:T(2,128)(2,1)S(1)} %reshape.429, f32[2,3,640,128]{2,3,1,0:T(8,128)S(1)} %fusion.88, f32[2,3,640,512]{2,3,1,0:T(8,128)} %copy-done.7, ...), kind=kOutput, calls=%fused_computation.14 | convolution fusion | flops 658641280 | bytes 15745280 | tf_op jit(solution)/shard_map/sub | solution.py:260
  691.9 70.9 %all-reduce.18.cloned.1.call-done = f32[2,640,768]{2,1,0:T(8,128)} async-done(((f32[2,640,768]{2,1,0:T(8,128)}), f32[2,640,768]{2,1,0:T(8,128)}) %all-reduce.18.cloned.1.call-update) | async-done | bytes 3932176 | tf_op jit(solution)/shard_map/psum | solution.py:314
  773.0 7.3 fusion.54
  780.4 6.6 scatter_custom_fusion.1
  789.4 39.9 %all-reduce.1 = (f32[768]{0:T(1024)}, f32[768]{0:T(1024)}, f32[768]{0:T(1024)}, f32[768]{0:T(1024)}, f32[256]{0:T(256)}) all-reduce(f32[768]{0:T(1024)S(1)} %copy-done.94, f32[768]{0:T(1024)S(1)} %copy-done.95, f32[768]{0:T(1024)S(1)} %copy-done.90, f32[768]{0:T(1024)S(1)} %reduce_sum.266, ...), channel_id=1, replica_groups=mesh['dp'=8,'mp'=4] {'dp'}, use_global_device_ids=true, to_apply=%region_37.38 | all-reduce | flops 3328 | bytes 26624 | tf_op jit(solution)/shard_map/psum | solution.py:345
  829.8 12.5 %scatter_fusion.1 = bf16[8,64,64]{2,1,0:T(8,128)(2,1)S(1)} fusion(bf16[8,64,64]{2,1,0:T(8,128)(2,1)S(1)} %broadcast.391, s32[256]{0:T(256)S(1)} %bitcast.216, bf16[256,64]{1,0:T(8,128)(2,1)S(1)} %copy.100), kind=kCustom, calls=%fused_computation.5 | custom fusion | bytes 100352 | tf_op jit(solution)/shard_map/scatter | solution.py:326
  854.5 7.2 scatter_fusion.2
  865.5 220.0 %all-reduce.20.cloned.1.call-done = (f32[64,768]{1,0:T(8,128)}, f32[4,768,192]{1,2,0:T(8,128)}, f32[768,192]{0,1:T(8,128)}, f32[768,192]{0,1:T(8,128)}, f32[192,...) async-done(((f32[64,768]{1,0:T(8,128)}, f32[4,768,192]{1,2,0:T(8,128)}, f32[768,192]{0,1:T(8,128)}, f32[768,192]{0,1:T(8,128)}, ...) | async-done | bytes 9830416 | tf_op jit(solution)/shard_map/psum | solution.py:345
  (435 shorter events, 241.2 us)
Async XLA Ops:
  7.2 212.0 %copy-start = (bf16[768,768]{1,0:T(8,128)(2,1)S(1)}, bf16[768,768]{1,0:T(8,128)(2,1)}, u32[]{:S(2)}) copy-start(bf16[768,768]{1,0:T(8,128)(2,1)} %param.42) | copy-start | bytes 3538948
  8.9 52.7 %copy-start.8 = (s32[256,1]{0,1:T(1,128)}, s32[256,1]{0,1:T(1,128)S(1)}, u32[]{:S(2)}) copy-start(s32[256,1]{0,1:T(1,128)S(1)} %get-tuple-element.355) | copy-start | bytes 3076
  48.2 13.6 %all-to-all-start = ((s32[8,1,64]{2,1,0:T(1,128)}), s32[8,1,64]{2,1,0:T(1,128)S(1)}, u32[]{:S(2)}, u32[]{:S(2)}) async-start(s32[8,1,64]{2,1,0:T(1,128)} %bitcast.9), calls=%async_computation | async-start | bytes 8192 | tf_op jit(solution)/shard_map/all_to_all | solution.py:102
  58.8 55.1 %copy-start.15 = (bf16[2,512,768]{2,1,0:T(8,128)(2,1)S(1)}, bf16[2,512,768]{2,1,0:T(8,128)(2,1)}, u32[]{:S(2)}) copy-start(bf16[2,512,768]{2,1,0:T(8,128)(2,1)} %param.27) | copy-start | bytes 4718596
  61.9 53.7 %copy-start.97 = (pred[8,64]{1,0:T(8,128)(4,1)}, pred[8,64]{1,0:T(8,128)(4,1)S(1)}, u32[]{:S(2)}) copy-start(pred[8,64]{1,0:T(8,128)(4,1)S(1)} %get-tuple-element.363) | copy-start | bytes 1540
  62.0 53.6 %copy-start.80 = (s32[512]{0:T(512)}, s32[512]{0:T(512)S(1)}, u32[]{:S(2)}) copy-start(s32[512]{0:T(512)S(1)} %reshape.437) | copy-start | bytes 6148
  65.9 12.7 %all-to-all-start.1 = ((bf16[8,2,2048]{2,1,0:T(2,128)(2,1)}), bf16[8,2,2048]{2,1,0:T(2,128)(2,1)S(1)}, u32[]{:S(2)}, u32[]{:S(2)}) async-start(bf16[8,2,2048]{2,1,0:T(2,128)(2,1)} %reshape.525), calls=%async_computation.1 | async-start | bytes 131072 | tf_op jit(solution)/shard_map/all_to_all | solution.py:106
  71.7 42.2 %all-reduce.10.cloned.1.call-start = ((), (), s32[]{:S(2)}) async-start(), calls=%async_computation.4 | async-start | bytes 1572864 | tf_op jit(solution)/shard_map/psum | solution.py:108
  71.8 53.6 %copy-start.84 = (pred[2,640]{1,0:T(4,128)(4,1)}, pred[2,640]{1,0:T(4,128)(4,1)S(1)}, u32[]{:S(2)}) copy-start(pred[2,640]{1,0:T(4,128)(4,1)S(1)} %concatenate.52) | copy-start | bytes 3844
  81.5 132.0 %all-reduce.12.cloned.1.call-start = ((), (), s32[]{:S(2)}) async-start(), calls=%async_computation.5 | async-start | bytes 7864320 | tf_op jit(solution)/shard_map/psum | solution.py:152
  132.1 184.5 %all-reduce.14.cloned.1.call-start = ((), (), s32[]{:S(2)}) async-start(), calls=%async_computation.6 | async-start | bytes 7864320 | tf_op jit(solution)/shard_map/psum | solution.py:159
  235.2 123.7 %all-gather.7.cloned.1.call-start = ((), (), s32[]{:S(2)}) async-start(), calls=%async_computation.7 | async-start | bytes 5160960 | tf_op jit(solution)/shard_map/all_gather | solution.py:171
  235.7 296.0 %reduce-scatter.2.cloned.1.call-start = ((), (), s32[]{:S(2)}) async-start(), calls=%async_computation.8 | async-start | bytes 294912 | tf_op jit(solution)/shard_map/reduce_scatter | solution.py:228
  473.8 163.7 %all-reduce.16.cloned.1.call-start = ((), (), s32[]{:S(2)}) async-start(), calls=%async_computation.9 | async-start | bytes 7864320 | tf_op jit(solution)/shard_map/psum | solution.py:244
  557.1 205.7 %all-reduce.18.cloned.1.call-start = ((), (), s32[]{:S(2)}) async-start(), calls=%async_computation.10 | async-start | bytes 7864320 | tf_op jit(solution)/shard_map/psum | solution.py:314
  562.6 74.9 %copy-start.77 = (f32[768]{0:T(1024)S(1)}, f32[768]{0:T(1024)}, u32[]{:S(2)}) copy-start(f32[768]{0:T(1024)} %param.40) | copy-start | bytes 9220
  566.0 77.8 %copy-start.73 = (f32[1280]{0:T(1024)S(1)}, f32[1280]{0:T(1024)}, u32[]{:S(2)}) copy-start(f32[1280]{0:T(1024)} %copy-done.72) | copy-start | bytes 15364
  681.3 404.2 %all-reduce.20.cloned.1.call-start = ((), (), s32[]{:S(2)}) async-start(), calls=%async_computation.11 | async-start | bytes 19660800 | tf_op jit(solution)/shard_map/psum | solution.py:345
  787.0 59.5 %copy-start.107 = (s32[2,128]{1,0:T(2,128)S(1)}, s32[2,128]{1,0:T(2,128)}, u32[]{:S(2)}) copy-start(s32[2,128]{1,0:T(2,128)} %copy-done.106) | copy-start | bytes 3076
  787.0 59.5 %copy-start.109 = (s32[2,128]{1,0:T(2,128)S(1)}, s32[2,128]{1,0:T(2,128)}, u32[]{:S(2)}) copy-start(s32[2,128]{1,0:T(2,128)} %copy-done.108) | copy-start | bytes 3076
  787.0 59.5 %copy-start.111 = (f32[2,128]{1,0:T(2,128)S(1)}, f32[2,128]{1,0:T(2,128)}, u32[]{:S(2)}) copy-start(f32[2,128]{1,0:T(2,128)} %copy-done.110) | copy-start | bytes 3076
  789.4 65.0 %copy-start.98 = (pred[8,64]{1,0:T(8,128)(4,1)S(1)}, pred[8,64]{1,0:T(8,128)(4,1)}, u32[]{:S(2)}) copy-start(pred[8,64]{1,0:T(8,128)(4,1)} %copy-done.97) | copy-start | bytes 1540
  789.4 65.1 %copy-start.81 = (s32[512]{0:T(512)S(1)}, s32[512]{0:T(512)}, u32[]{:S(2)}) copy-start(s32[512]{0:T(512)} %copy-done.80) | copy-start | bytes 6148
  843.1 11.1 %all-to-all-start.2 = ((bf16[8,2,2048]{2,1,0:T(2,128)(2,1)}), bf16[8,2,2048]{2,1,0:T(2,128)(2,1)S(1)}, u32[]{:S(2)}, u32[]{:S(2)}) async-start(bf16[8,2,2048]{2,1,0:T(2,128)(2,1)} %reshape.527), calls=%async_computation.3 | async-start | bytes 131072 | tf_op jit(solution)/shard_map/all_to_all | solution.py:327
  (110 other events, 760.0 us)
Sparse Core Ops, SparseCore 0:
  81.6 32.2 all-reduce.9
  132.2 81.2 all-reduce.11
  235.3 81.3 all-reduce.13
  318.1 34.2 all-gather.6
  473.9 57.7 reduce-scatter.1
  557.2 80.2 all-reduce.15
  681.4 81.3 all-reduce.17
  769.9 315.5 all-reduce.19
where the time goes:
time: 1110 us; the launch traced here: 1100 us
  waiting for transfers between devices  605 us (55%)
  local copies, waits for them, and re-layouts  133 us (12%)
  blocking collectives  128 us (12%)
  matrix products  114 us (10%)
  other arithmetic  91.9 us (8%)
  starting transfers between devices  17.3 us (2%)
  between operations  16 us (1%)
    psum x1, waiting for transfers between devices, shards(): lax.psum((grad_query, grad_key, grad_value, grad_out, grad_gain_attn, gra...  220 us
    psum x1, waiting for transfers between devices, shards(): attn_sum = lax.psum(matmul(context, w_out), 'mp')  78.4 us
    psum x1, waiting for transfers between devices, shards(): lax.psum(contract_product('tf,df->td', d_pre_act, w_up), 'mp')  71.5 us
    psum x1, waiting for transfers between devices, shards(): d_stream_sum = lax.psum(d_stream, 'mp')  70.9 us
    psum x1, waiting for transfers between devices, shards(): ffn_sum = lax.psum(matmul(hidden, w_down), 'mp')  69.9 us
    dot_general x37, matrix products, contract_product(): jnp.einsum(form, first_op, second_op, preferred_element_type=jnp.float32)  67.5 us
    all_gather x3, blocking collectives, combined_all(): gathered = jax.tree.map(lambda a: lax.all_gather(a, axis), part)  55.3 us
    reduce_scatter x1, waiting for transfers between devices, shards(): lax.psum_scatter(grad_head_vec, 'dp', scatter_dimension=0, tiled=True)  54.1 us
  transfers between devices with their start and end apart: 11, of which 10 were waited for; matrix products, arithmetic and copies ran while one was open for 9% of the time, Pallas kernels for 0%

commit v1 on v0

v1 whole, which is shorter than its diff:
```python
import functools
import math

import jax
import jax.numpy as jnp
from jax import lax
from jax.experimental import pallas as pl
from jax.experimental.pallas import tpu as pltpu
from jax.sharding import PartitionSpec as P

DH = 64
SPANW = 4
EPSILON = 1e-05
MASKED_SCORE = -1000000000.0
LANES = 128
BF = jnp.bfloat16
F32 = jnp.float32
MESH = pl.DeviceIdType.MESH
VM = pl.BlockSpec(memory_space=pltpu.VMEM)


def matmul(first_op, second_op):
    return jnp.dot(first_op, second_op, preferred_element_type=F32)


def contract_product(form, first_op, second_op):
    return jnp.einsum(form, first_op, second_op, preferred_element_type=F32)


def normalize(source, gain_vec, shift_vec):
    center = source - jnp.mean(source, axis=-1, keepdims=True)
    inv_scale = lax.rsqrt(jnp.mean(center * center, axis=-1, keepdims=True) + EPSILON)
    return center * inv_scale * gain_vec + shift_vec


def gelu_exact(source):
    return jax.nn.gelu(source, approximate=False)


def head_map(head_pre, gain_vec):
    return normalize(gelu_exact(head_pre), gain_vec, 0.0)


def remote(src, dst, send, recv, axis, peer):
    return pltpu.make_async_remote_copy(
        src_ref=src, dst_ref=dst, send_sem=send, recv_sem=recv,
        device_id={axis: peer}, device_id_type=MESH,
    )


def exchange_kernel(axis, n, kinds, *refs):
    k = len(kinds)
    ins, outs, (send_sems, recv_sems, own_sems) = refs[:k], refs[k:2 * k], refs[2 * k:]
    me = lax.axis_index(axis)
    barrier = pltpu.get_barrier_semaphore()

    def greet(step, carry):
        pl.semaphore_signal(
            barrier, inc=1, device_id={axis: lax.rem(me + step, n)}, device_id_type=MESH
        )
        return carry

    lax.fori_loop(1, n, greet, 0)
    own = []
    for i, kind in enumerate(kinds):
        src = ins[i].at[me] if kind == "a2a" else ins[i]
        own.append(pltpu.make_async_copy(src, outs[i].at[me], own_sems.at[i]))
        own[-1].start()
    pl.semaphore_wait(barrier, n - 1)

    def copies(step):
        peer = lax.rem(me + step, n)
        return [
            remote(
                ins[i].at[peer] if kind == "a2a" else ins[i], outs[i].at[me],
                send_sems.at[i, step - 1], recv_sems.at[i, step - 1], axis, peer,
            )
            for i, kind in enumerate(kinds)
        ]

    def begin(step, carry):
        for copy in copies(step):
            copy.start()
        return carry

    lax.fori_loop(1, n, begin, 0)

    def finish(step, carry):
        source = lax.rem(me + n - step, n)
        for i, kind in enumerate(kinds):
            remote(
                ins[i].at[source] if kind == "a2a" else ins[i], outs[i].at[source],
                send_sems.at[i, step - 1], recv_sems.at[i, step - 1], axis, source,
            ).wait()
        return carry

    lax.fori_loop(1, n, finish, 0)
    for copy in own:
        copy.wait()


def exchange(axis, collective, arrays):
    n = lax.axis_size(axis)
    kinds = tuple(kind for kind, _ in arrays)
    values = [value for _, value in arrays]
    shapes = [
        jax.ShapeDtypeStruct(value.shape if kind == "a2a" else (n,) + value.shape, value.dtype)
        for kind, value in arrays
    ]
    k = len(values)
    return pl.pallas_call(
        functools.partial(exchange_kernel, axis, n, kinds),
        out_shape=shapes,
        in_specs=[VM] * k,
        out_specs=[VM] * k,
        scratch_shapes=[
            pltpu.SemaphoreType.DMA((k, n - 1)),
            pltpu.SemaphoreType.DMA((k, n - 1)),
            pltpu.SemaphoreType.DMA((k,)),
        ],
        compiler_params=pltpu.CompilerParams(collective_id=collective, has_side_effects=True),
    )(*values)


def sum_kernel(chunks, x_ref, o_ref, r1, s2, r2, send_sems, recv_sems):
    me = lax.axis_index("mp")
    b0 = lax.rem(me, 2)
    b1 = me // 2
    p1 = me + 1 - 2 * b0
    p2 = lax.rem(me + 2, 4)
    half = r1.shape[1]
    quarter = half // 2
    barrier = pltpu.get_barrier_semaphore()
    for peer in (p1, p2):
        pl.semaphore_signal(barrier, inc=1, device_id={"mp": peer}, device_id_type=MESH)
    pl.semaphore_wait(barrier, 2)

    def rows(c, h, q, count):
        return pl.ds(pl.multiple_of(c * 2 * half + h * half + q * quarter, 16), count)

    def first(c):
        return remote(
            x_ref.at[rows(c, 1 - b0, 0, half)], r1.at[c], send_sems.at[c, 0], recv_sems.at[c, 0],
            "mp", p1,
        )

    def second(c):
        return remote(s2.at[c], r2.at[c], send_sems.at[c, 1], recv_sems.at[c, 1], "mp", p2)

    def third(c, q):
        place = o_ref.at[rows(c, b0, q, quarter)]
        return remote(place, place, send_sems.at[c, 2], recv_sems.at[c, 2], "mp", p2)

    def fourth(c, h):
        place = o_ref.at[rows(c, h, b1, quarter)]
        return remote(place, place, send_sems.at[c, 3], recv_sems.at[c, 3], "mp", p1)

    def fifth(c, h):
        place = o_ref.at[rows(c, h, 1 - b1, quarter)]
        return remote(place, place, send_sems.at[c, 4], recv_sems.at[c, 4], "mp", p1)

    def part(c, q):
        mine = x_ref[rows(c, b0, q, quarter)].astype(F32)
        theirs = r1[c, pl.ds(pl.multiple_of(q * quarter, 16), quarter)].astype(F32)
        return mine + theirs

    for c in range(chunks):
        first(c).start()
    for c in range(chunks):
        first(c).wait_recv()
        s2[c] = part(c, 1 - b1).astype(BF)
        second(c).start()
    for c in range(chunks):
        own = part(c, b1)
        second(c).wait_recv()
        o_ref[rows(c, b0, b1, quarter)] = (own + r2[c].astype(F32)).astype(BF)
        third(c, b1).start()
        fourth(c, b0).start()
    for c in range(chunks):
        third(c, 1 - b1).wait_recv()
        fifth(c, b0).start()
    for c in range(chunks):
        fourth(c, 1 - b0).wait_recv()
        fifth(c, 1 - b0).wait_recv()
        first(c).wait_send()
        second(c).wait_send()
        third(c, b1).wait_send()
        fourth(c, b0).wait_send()
        fifth(c, b0).wait_send()


def sum_mp(part, collective, chunks=2):
    total, width = part.shape
    half = total // chunks // 2
    return pl.pallas_call(
        functools.partial(sum_kernel, chunks),
        out_shape=jax.ShapeDtypeStruct((total, width), BF),
        in_specs=[VM],
        out_specs=VM,
        scratch_shapes=[
            pltpu.VMEM((chunks, half, width), BF),
            pltpu.VMEM((chunks, half // 2, width), BF),
            pltpu.VMEM((chunks, half // 2, width), BF),
            pltpu.SemaphoreType.DMA((chunks, 5)),
            pltpu.SemaphoreType.DMA((chunks, 5)),
        ],
        compiler_params=pltpu.CompilerParams(collective_id=collective, has_side_effects=True),
    )(part.astype(BF))


def shards(
    words, word_extra, span_pos, span_len, entity_shard, entity_row, targets, table, ent_proj,
    query_weight, w_key, w_value, w_out, gain_attn, bias_attn, w_up, w_down, gain_ffn, bias_ffn,
    w_head, gain_head, cot_words, cot_ents,
):
    n_dp = lax.axis_size("dp")
    n_mp = lax.axis_size("mp")
    seq_count, word_length, model_width = words.shape
    ent_len = span_pos.shape[1]
    masked_len = targets.shape[1]
    tokens_len = word_length + ent_len
    rows_dev, cols_dev = table.shape
    local_width = w_key.shape[1]
    heads_local = local_width // DH
    ent_total = seq_count * ent_len
    table_full = lax.all_gather(table, "mp", axis=1, tiled=True)

    owners = entity_shard.reshape(ent_total)
    wanted = entity_row.reshape(ent_total)
    capacity = max(16, 2 * ent_total // n_dp)
    owner_onehot = (owners[:, None] == jnp.arange(n_dp, dtype=jnp.int32)[None, :]).astype(BF)
    order_index = jnp.arange(ent_total, dtype=jnp.int32)
    earlier = (order_index[:, None] > order_index[None, :]).astype(BF)
    before = matmul(earlier, owner_onehot)
    slot_rank = jnp.sum(before * owner_onehot.astype(F32), axis=1).astype(jnp.int32)
    place = owners * capacity + slot_rank
    placed = place[:, None] == jnp.arange(n_dp * capacity, dtype=jnp.int32)[None, :]
    requests = jnp.sum(jnp.where(placed, wanted[:, None] + 1, 0), axis=0) - 1
    requests = jnp.pad(requests.reshape(n_dp, 1, capacity), ((0, 0), (0, 7), (0, LANES - capacity)))
    (received,) = exchange("dp", 0, [("a2a", requests)])
    received = received[:, 0, :capacity]
    present = received >= 0
    picked = jnp.take(table, jnp.maximum(received, 0), axis=0)
    picked = jnp.where(present[..., None], picked, jnp.zeros_like(picked))
    (back_rows,) = exchange("dp", 1, [("a2a", picked)])
    placed_low = placed.astype(BF)
    vec_cols = matmul(placed_low, back_rows.reshape(n_dp * capacity, cols_dev)).astype(BF)
    vec_all, proj_all = exchange("mp", 2, [("ag", vec_cols), ("ag", ent_proj)])
    ent_vectors = contract_product("mtc,mcd->td", vec_all, proj_all)

    word_count = word_length // 8 + word_extra
    span_start = span_pos * (word_count[:, None] - SPANW) // word_length
    positions = jnp.arange(word_length, dtype=jnp.int32)
    inside = (positions[None, None, :] >= span_start[..., None]) & (
        positions[None, None, :] < (span_start + span_len)[..., None]
    )
    span_total = contract_product("sep,spd->sed", inside.astype(BF), words)
    span_width = span_len.astype(F32)[..., None]
    ent_low = (
        ent_vectors.reshape(seq_count, ent_len, model_width) + span_total / span_width
    ).astype(BF)
    stream = jnp.concatenate([words, ent_low], axis=1)
    word_query = contract_product("rpa,gay->grpy", words, query_weight[:2])
    q_ent = contract_product("sed,kdh->kseh", ent_low, query_weight[2:])
    to_words = jnp.concatenate([word_query[0], q_ent[0]], axis=1).astype(BF)
    to_ents = jnp.concatenate([word_query[1], q_ent[1]], axis=1).astype(BF)
    key_rows = contract_product("snd,dh->snh", stream, w_key).astype(BF)
    value_rows = contract_product("snd,dh->snh", stream, w_value).astype(BF)
    head_shape = (seq_count, tokens_len, heads_local, DH)
    words_heads = to_words.reshape(head_shape)
    ents_heads = to_ents.reshape(head_shape)
    keys_heads = key_rows.reshape(head_shape)
    values_heads = value_rows.reshape(head_shape)
    key_valid = jnp.concatenate(
        [positions[None, :] < word_count[:, None], jnp.ones((seq_count, ent_len), dtype=bool)],
        axis=1,
    )

    def score_rows():
        word_part = contract_product("sqhc,skhc->shqk", words_heads, keys_heads[:, :word_length])
        ent_part = contract_product("sqhc,skhc->shqk", ents_heads, keys_heads[:, word_length:])
        raw_scores = jnp.concatenate([word_part, ent_part], axis=-1) * 0.125
        return jnp.where(key_valid[:, None, None, :], raw_scores, MASKED_SCORE)

    scores = score_rows()
    row_max = jnp.max(scores, axis=-1, keepdims=True)
    log_total = row_max + jnp.log(jnp.sum(jnp.exp(scores - row_max), axis=-1, keepdims=True))
    prob_low = jnp.exp(scores - log_total).astype(BF)
    context = (
        contract_product("shqk,skhc->sqhc", prob_low, values_heads)
        .reshape(seq_count * tokens_len, local_width)
        .astype(BF)
    )
    attn_sum = sum_mp(matmul(context, w_out), 3).astype(F32)
    pre_first = stream.reshape(seq_count * tokens_len, model_width).astype(F32) + attn_sum
    first_norm, first_back = jax.vjp(normalize, pre_first, gain_attn, bias_attn)
    first_low = first_norm.astype(BF)
    pre_act = matmul(first_low, w_up)
    hidden_f, gelu_back = jax.vjp(gelu_exact, pre_act)
    hidden = hidden_f.astype(BF)
    ffn_sum = sum_mp(matmul(hidden, w_down), 4).astype(F32)
    pre_second = first_norm + ffn_sum
    output, second_back = jax.vjp(normalize, pre_second, gain_ffn, bias_ffn)
    out_low = output.astype(BF).reshape(seq_count, tokens_len, model_width)
    out_words = out_low[:, :word_length]
    out_ents = out_low[:, word_length:]
    head_in = out_low[:, word_length : word_length + masked_len].reshape(
        seq_count * masked_len, model_width
    )
    head_pre = matmul(head_in, w_head)
    head_vec, head_back = jax.vjp(head_map, head_pre, gain_head)
    (all_head,) = exchange("dp", 5, [("ag", head_vec.astype(BF))])
    mine_total = head_vec.shape[0]
    masked_total = n_dp * mine_total
    ent_width = table_full.shape[1]
    all_head = all_head.reshape(masked_total, ent_width)
    row_offset = lax.axis_index("dp") * rows_dev
    local_target = targets.reshape(-1) - row_offset
    is_mine = (local_target >= 0) & (local_target < rows_dev)
    target_index = jnp.clip(local_target, 0, rows_dev - 1)
    target_rows = jnp.where(
        is_mine[:, None], jnp.take(table_full, target_index, axis=0), jnp.zeros((), BF)
    )
    target_logit = jnp.sum(all_head.astype(F32) * target_rows.astype(F32), axis=-1)
    block_rows = math.gcd(masked_total, 256)
    block_count = masked_total // block_rows
    head_blocks = all_head.reshape(block_count, block_rows, ent_width)

    def logits_of(head_block):
        return contract_product("md,rd->mr", head_block, table_full)

    def block_part(head_block):
        logits = logits_of(head_block)
        row_top = jnp.max(logits, axis=1)
        weights = jnp.exp(logits - row_top[:, None])
        return row_top, jnp.sum(weights, axis=1), matmul(weights.astype(BF), table_full)

    if block_count == 1:
        parts = [a[None] for a in block_part(head_blocks[0])]
    else:
        parts = lax.map(block_part, head_blocks)
    part_top, part_total = parts[0].reshape(masked_total), parts[1].reshape(masked_total)
    stats = jnp.zeros((8, masked_total), F32)
    stats = stats.at[0].set(part_top).at[1].set(part_total).at[2].set(target_logit)
    all_stats, all_parts, all_rows = exchange(
        "dp", 6,
        [
            ("ag", stats),
            ("a2a", parts[2].reshape(n_dp, mine_total, ent_width)),
            ("a2a", target_rows.reshape(n_dp, mine_total, ent_width)),
        ],
    )
    global_top = jnp.max(all_stats[:, 0], axis=0)
    shrink = jnp.exp(all_stats[:, 0] - global_top)
    global_total = jnp.sum(shrink * all_stats[:, 1], axis=0)
    head_total = global_top + jnp.log(global_total)
    loss = head_total - jnp.sum(all_stats[:, 2], axis=0)
    weight_all = shrink / global_total
    my_slots = lax.axis_index("dp") * mine_total
    my_weight = lax.dynamic_slice_in_dim(weight_all, my_slots, mine_total, 1)
    grad_head_mine = jnp.sum(
        all_parts * my_weight[..., None] - all_rows.astype(F32), axis=0
    )
    my_cols = lax.dynamic_slice_in_dim(all_head, lax.axis_index("mp") * cols_dev, cols_dev, 1)

    def block_back(running, inputs):
        head_block, col_block, total_block = inputs
        weight_low = jnp.exp(logits_of(head_block) - total_block[:, None]).astype(BF)
        return running + contract_product("mr,mc->rc", weight_low, col_block), None

    d_head_pre, grad_gain_head = head_back(grad_head_mine)
    d_head_low = d_head_pre.astype(BF)
    grad_head = contract_product("md,me->de", head_in, d_head_low)
    d_head_in = contract_product("me,de->md", d_head_low, w_head)
    d_output = jnp.concatenate([cot_words, cot_ents], axis=1).astype(F32)
    d_output = d_output.at[:, word_length : word_length + masked_len].add(
        d_head_in.reshape(seq_count, masked_len, model_width)
    )
    d_output = d_output.reshape(seq_count * tokens_len, model_width)
    d_second, grad_gain_ffn, grad_bias_ffn = second_back(d_output)
    d_ffn = d_second.astype(BF)
    grad_down = contract_product("tf,td->fd", hidden, d_ffn)
    d_hidden = contract_product("td,fd->tf", d_ffn, w_down)
    d_pre_act = gelu_back(d_hidden)[0].astype(BF)
    grad_up = contract_product("td,tf->df", first_low, d_pre_act)
    early = lax.psum(
        (grad_down.astype(BF), grad_up.astype(BF), grad_head.astype(BF)), "dp"
    )
    d_first = d_second + sum_mp(contract_product("tf,df->td", d_pre_act, w_up), 7).astype(F32)
    d_pre_first, grad_gain_attn, grad_bias_attn = first_back(d_first)
    d_attn = d_pre_first.astype(BF)
    grad_out = contract_product("th,td->hd", context, d_attn)
    d_context = contract_product("td,hd->th", d_attn, w_out).astype(BF).reshape(head_shape)
    prob_rows = jnp.exp(score_rows() - log_total)
    prob_again = prob_rows.astype(BF)
    d_probs = contract_product("sqhc,skhc->shqk", d_context, values_heads)
    d_values = (
        contract_product("shqk,sqhc->skhc", prob_again, d_context)
        .astype(BF)
        .reshape(seq_count, tokens_len, local_width)
    )
    d_scores = (
        prob_rows * (d_probs - jnp.sum(prob_rows * d_probs, axis=-1, keepdims=True))
    ).astype(BF)

    def bound(form, first_op, second_op):
        return (
            (contract_product(form, first_op, second_op) * 0.125)
            .astype(BF)
            .reshape(seq_count, -1, local_width)
        )

    d_score_words, d_score_ents = d_scores[..., :word_length], d_scores[..., word_length:]
    d_to_words = bound("shqk,skhc->sqhc", d_score_words, keys_heads[:, :word_length])
    d_to_ents = bound("shqk,skhc->sqhc", d_score_ents, keys_heads[:, word_length:])
    d_keys = jnp.concatenate(
        [
            bound("shqk,sqhc->skhc", d_score_words, words_heads),
            bound("shqk,sqhc->skhc", d_score_ents, ents_heads),
        ],
        axis=1,
    )
    grad_query = jnp.stack(
        [
            contract_product("yir,yiq->rq", words, d_to_words[:, :word_length]),
            contract_product("yir,yiq->rq", words, d_to_ents[:, :word_length]),
            contract_product("sed,seh->dh", ent_low, d_to_words[:, word_length:]),
            contract_product("sed,seh->dh", ent_low, d_to_ents[:, word_length:]),
        ]
    )
    grad_key = contract_product("snd,snh->dh", stream, d_keys)
    grad_value = contract_product("snd,snh->dh", stream, d_values)
    d_stream_word = contract_product(
        "vcr,er->vce", d_to_words[:, :word_length], query_weight[0]
    ) + contract_product("vcr,er->vce", d_to_ents[:, :word_length], query_weight[1])
    d_stream_ent = contract_product(
        "seh,dh->sed", d_to_words[:, word_length:], query_weight[2]
    ) + contract_product("seh,dh->sed", d_to_ents[:, word_length:], query_weight[3])
    d_stream = (
        jnp.concatenate([d_stream_word, d_stream_ent], axis=1)
        + contract_product("snh,dh->snd", d_keys, w_key)
        + contract_product("snh,dh->snd", d_values, w_value)
    )
    d_stream_sum = sum_mp(d_stream.reshape(seq_count * tokens_len, model_width), 8).astype(F32)
    d_total = (d_pre_first + d_stream_sum).reshape(seq_count, tokens_len, model_width)
    d_ent = d_total[:, word_length:].astype(BF)
    grad_words = d_total[:, :word_length] + contract_product(
        "sep,sed->spd", inside.astype(BF), (d_ent.astype(F32) / span_width).astype(BF)
    )
    d_ent_flat = d_ent.reshape(ent_total, model_width)
    grad_ent_proj = contract_product("tc,td->cd", vec_cols, d_ent_flat)
    d_vec = contract_product("td,cd->tc", d_ent_flat, ent_proj).astype(BF)
    outbox = contract_product("tp,tc->pc", placed_low, d_vec).astype(BF)
    (inbox,) = exchange("dp", 9, [("a2a", outbox.reshape(n_dp, capacity, cols_dev))])

    table_grad, _ = lax.scan(
        block_back,
        jnp.zeros((rows_dev, cols_dev), F32),
        (
            head_blocks,
            my_cols.reshape(block_count, block_rows, cols_dev),
            head_total.reshape(block_count, block_rows),
        ),
    )
    row_index = jnp.arange(rows_dev, dtype=jnp.int32)
    hit = jnp.concatenate([received.reshape(-1), jnp.where(is_mine, local_target, -1)])
    hit_rows = jnp.concatenate([inbox.reshape(-1, cols_dev), -my_cols])
    table_grad = table_grad + contract_product(
        "tr,tc->rc", (hit[:, None] == row_index[None, :]).astype(BF), hit_rows
    )
    late, early = lax.optimization_barrier(
        (
            (
                grad_query.astype(BF), grad_key.astype(BF), grad_value.astype(BF),
                grad_out.astype(BF), grad_ent_proj.astype(BF),
            ),
            early,
        )
    )
    late = lax.psum(late, "dp")
    small = lax.psum(
        (grad_gain_attn, grad_bias_attn, grad_gain_ffn, grad_bias_ffn, grad_gain_head), "dp"
    )
    grad_down, grad_up, grad_head = (a.astype(F32) for a in early)
    grad_query, grad_key, grad_value, grad_out, grad_ent_proj = (a.astype(F32) for a in late)
    grad_gain_attn, grad_bias_attn, grad_gain_ffn, grad_bias_ffn, grad_gain_head = small
    return (
        out_words, out_ents, loss, grad_words, table_grad, grad_ent_proj, grad_query, grad_key,
        grad_value, grad_out, grad_gain_attn, grad_bias_attn, grad_up, grad_down, grad_gain_ffn,
        grad_bias_ffn, grad_head, grad_gain_head,
    )


def solution(mesh):
    return jax.shard_map(
        shards,
        mesh=mesh,
        in_specs=(
            P("dp", None, None), P("dp"), P("dp", None), P("dp", None), P("dp", None, None),
            P("dp", None), P(), P("dp", "mp"), P("mp", None), P(None, None, "mp"), P(None, "mp"),
            P(None, "mp"), P("mp", None), P(), P(), P(None, "mp"), P("mp", None), P(), P(), P(),
            P(), P("dp", None, None), P("dp", None, None),
        ),
        out_specs=(
            P("dp", None, None), P("dp", None, None), P(), P("dp", None, None), P("dp", "mp"),
            P("mp", None), P(None, None, "mp"), P(None, "mp"), P(None, "mp"), P("mp", None), P(),
            P(), P(None, "mp"), P("mp", None), P(), P(), P(), P(),
        ),
        check_vma=False,
    )
```

time: 1110 us -> 595 us (0.54)
  waiting for transfers between devices: 605 us -> 111 us
  Pallas kernels: 0 us -> 181 us
  local copies, waits for them, and re-layouts: 133 us -> 44.8 us
  blocking collectives: 128 us -> 40.5 us
  other arithmetic: 91.9 us -> 73.1 us
  starting transfers between devices: 17.3 us -> 0.12 us
    psum x6 -> x2, waiting for transfers between devices: 541 us -> 111 us  [the longest x1 75.1 us: shards(): lax.psum((grad_down.astype(BF), grad_up.astype(BF), grad_head.astype(BF))...]
    pallas_call x0 -> x10, Pallas kernels: none -> 181 us  [the longest x4 120 us: sum_mp(): pl.pallas_call(functools.partial(sum_kernel, chunks), out_shape=jax.Shape...]
    all_gather x4 -> x0, blocking collectives: 87.9 us -> none  [the longest x3 55.3 us: combined_all(): gathered = jax.tree.map(lambda a: lax.all_gather(a, axis), part)]
    reduce_scatter x1 -> x0, waiting for transfers between devices: 54.1 us -> none  [shards(): lax.psum_scatter(grad_head_vec, 'dp', scatter_dimension=0, tiled=True)]
    scatter x2 -> x3, local copies, waits for them, and re-layouts: 51.2 us -> 3.19 us  [shards(): stats.at[0].set(part_top).at[1].set(part_total).at[2].set(target_logit)]
    unnamed x264 -> x253, local copies, waits for them, and re-layouts: 43.3 us -> 17.5 us
    add x15 -> x3, other arithmetic: 21.4 us -> 4.7 us  [the longest x1 3.33 us: shards(): d_pre_first + d_stream_sum]
    all_to_all x3 -> x0, starting transfers between devices: 16.4 us -> none  [the longest x1 7.25 us: shards(): lax.all_to_all(requests, 'dp', split_axis=0, concat_axis=0, tiled=True)]
  transfers between devices with their start and end apart: 11 -> 3, of which waited for: 10 -> 2; matrix products, arithmetic and copies ran while one was open for 9% -> 19% of each run, Pallas kernels for 0% -> 23%
where the time goes in v1:
time: 595 us; the launch traced here: 586 us
  Pallas kernels  181 us (30%)
  matrix products  119 us (20%)
  waiting for transfers between devices  111 us (19%)
  other arithmetic  73.1 us (12%)
  local copies, waits for them, and re-layouts  44.8 us (8%)
  blocking collectives  40.5 us (7%)
  between operations  15.9 us (3%)
    pallas_call x4, Pallas kernels, sum_mp(): pl.pallas_call(functools.partial(sum_kernel, chunks), out_shape=jax.Shape...  120 us
    dot_general x40, matrix products, contract_product(): return jnp.einsum(form, first_op, second_op, preferred_element_type=F32)  78.9 us
    psum x1, waiting for transfers between devices, shards(): lax.psum((grad_down.astype(BF), grad_up.astype(BF), grad_head.astype(BF))...  75.1 us
    pallas_call x6, Pallas kernels, exchange(): pl.pallas_call(functools.partial(exchange_kernel, axis, n, kinds), out_sh...  61.4 us
    psum x1, blocking collectives, shards(): lax.psum((grad_gain_attn, grad_bias_attn, grad_gain_ffn, grad_bias_ffn, g...  40.5 us
    psum x1, waiting for transfers between devices, shards(): late = lax.psum(late, 'dp')  35.5 us
    dot_general x7, matrix products, matmul(): return jnp.dot(first_op, second_op, preferred_element_type=F32)  26.8 us
    unnamed x253, local copies, waits for them, and re-layouts  17.5 us
  transfers between devices with their start and end apart: 3, of which 2 were waited for; matrix products, arithmetic and copies ran while one was open for 19% of the time, Pallas kernels for 23%

profile of v1, /device:TPU:0, one launch (start us, length us, event | category | flops | bytes accessed | tf_op | source)
XLA Modules:
  0.0 586.2 jit_solution(3730995458299123569)
XLA Ops:
  11.2 9.8 %shard_map.358 = s32[8,8,128]{2,1,0:T(8,128)} custom-call(s32[8,8,128]{2,1,0:T(8,128)} %pad.14.refs_0_), custom_call_target="tpu_custom_call" | custom-call | tf_op jit(solution)/shard_map/pallas_call | solution.py:111
  29.8 8.9 %shard_map.359 = bf16[8,64,64]{2,1,0:T(8,128)(2,1)} custom-call(bf16[8,64,64]{2,1,0:T(8,128)(2,1)} %select_select_fusion.1.refs_0_), custom_call_target="tpu_custom_call" | custom-call | tf_op jit(solution)/shard_map/pallas_call | solution.py:111
  40.5 11.0 %shard_map.360 = (bf16[4,256,64]{2,1,0:T(8,128)(2,1)}, bf16[4,64,768]{2,1,0:T(8,128)(2,1)}) custom-call(bf16[256,64]{1,0:T(8,128)(2,1)} %convolution_convert_fusion.15.refs_0_, bf16[64,768]{1,0:T(8,128)(2,1)} %refs_1_.1), custom_call_target="tpu_custom_call" | custom-call | tf_op jit(solution)/shard_map/pallas_call | solution.py:111
  76.5 30.3 %shard_map.361 = bf16[1280,768]{1,0:T(8,128)(2,1)} custom-call(bf16[1280,768]{1,0:T(8,128)(2,1)} %convolution_convert_fusion.x_ref), custom_call_target="tpu_custom_call" | custom-call | tf_op jit(solution)/shard_map/pallas_call | solution.py:195
  111.2 11.5 %multiply_convert_fusion.1 = (bf16[1280,768]{1,0:T(8,128)(2,1)S(1)}, f32[1280,768]{1,0:T(8,128)}, f32[1280,768]{1,0:T(8,128)}) fusion(bf16[768,768]{1,0:T(8,128)(2,1)S(1)} %copy-done, f32[1280,768]{1,0:T(8,128)S(1)} %get-tuple-element.152, f32[768]{0:T(1024)S(1)} %copy-done.95, f32[768]{0:T(1024)S(1)} %copy-done.72, f32[1280]{0:T(1024)S(1)} %fusion.143), kind=kOutput, calls=%fused_computation.43 | convolution fusion | flops 1577779200 | bytes 14953472 | tf_op jit(solution)/shard_map/dot_general | solution.py:23
  127.0 30.1 %shard_map.362 = bf16[1280,768]{1,0:T(8,128)(2,1)} custom-call(bf16[1280,768]{1,0:T(8,128)(2,1)} %convolution_convert_fusion.2.x_ref), custom_call_target="tpu_custom_call" | custom-call | tf_op jit(solution)/shard_map/pallas_call | solution.py:195
  166.9 9.2 %shard_map.363 = bf16[8,32,256]{2,1,0:T(8,128)(2,1)} custom-call(bf16[32,256]{1,0:T(8,128)(2,1)} %multiply_convert_fusion.2.refs_0_), custom_call_target="tpu_custom_call" | custom-call | tf_op jit(solution)/shard_map/pallas_call | solution.py:111
  183.1 6.8 %copy.94 = bf16[8000,256]{1,0:T(8,128)(2,1)} copy(bf16[8000,256]{0,1:T(8,128)(2,1)} %all-gather.2.cloned.1.call-done) | data formatting | bytes 8192000 | tf_op jit(solution)/shard_map/all_gather | solution.py:226
  189.9 4.4 gather_fusion.1
  208.5 6.6 %fusion.11 = f32[256,256]{1,0:T(8,128)} fusion(bf16[8000,256]{0,1:T(8,128)(2,1)} %all-gather.2.cloned.1.call-done, f32[256,8000]{0,1:T(8,128)} %copy-done.2, f32[256]{0:T(256)} %copy-done.84), kind=kOutput, calls=%fused_computation.23 | convolution fusion | flops 1052672000 | bytes 12551168 | tf_op jit(solution)/shard_map/dot_general | solution.py:23
  215.1 14.1 %shard_map.364 = (f32[8,8,256]{2,1,0:T(8,128)}, f32[8,32,256]{2,1,0:T(8,128)}, bf16[8,32,256]{2,1,0:T(8,128)(2,1)}) custom-call(f32[8,256]{1,0:T(8,128)} %scatter.14.refs_0_, f32[8,32,256]{2,1,0:T(8,128)} %bitcast.240, bf16[8,32,256]{2,1,0:T(8,128)(2,1)} %get-tuple-element.141.refs_2_), custom_call_target="tpu_custom_call" | custom-call | tf_op jit(solution)/shard_map/pallas_call | solution.py:111
  239.7 5.3 fusion.18
  263.7 29.4 %shard_map.365 = bf16[1280,768]{1,0:T(8,128)(2,1)} custom-call(bf16[1280,768]{1,0:T(8,128)(2,1)} %convolution_convert_fusion.1.x_ref), custom_call_target="tpu_custom_call" | custom-call | tf_op jit(solution)/shard_map/pallas_call | solution.py:195
  293.2 5.5 multiply_reduce_fusion.1
  305.5 13.7 %multiply_convert_fusion = bf16[2,3,640,640]{2,3,1,0:T(8,128)(2,1)} fusion(f32[2,3,640]{2,1,0:T(4,128)S(1)} %copy-done.81, bf16[2,640,3,64]{1,3,2,0:T(8,128)(2,1)} %bitcast.270, bf16[2,640,3,64]{1,0,3,2:T(2,128)(2,1)S(1)} %reshape.492, f32[2,3,640,128]{2,3,1,0:T(8,128)S(1)} %fusion.102, f32[2,3,640,512]{2,3,1,0:T(8,128)} %copy-done.5, ...), kind=kOutput, calls=%fused_computation.8 | convolution fusion | flops 658641280 | bytes 15745280 | tf_op jit(solution)/shard_map/sub | solution.py:403
  339.1 5.1 fusion.17
  344.2 30.0 %shard_map.366 = bf16[1280,768]{1,0:T(8,128)(2,1)} custom-call(bf16[1280,768]{1,0:T(8,128)(2,1)} %bitcast.217), custom_call_target="tpu_custom_call" | custom-call | tf_op jit(solution)/shard_map/pallas_call | solution.py:195
  385.9 75.1 %all-reduce.11.cloned.1.call-done = (bf16[768,768]{1,0:T(8,128)(2,1)}, bf16[768,768]{1,0:T(8,128)(2,1)}, bf16[768,256]{1,0:T(8,128)(2,1)}) async-done(((bf16[768,768]{1,0:T(8,128)(2,1)}, bf16[768,768]{1,0:T(8,128)(2,1)}, bf16[768,256]{1,0:T(8,128)(2,1)}), (bf16[768,768]{1,0:T(8,128)(2,1)}, bf16[768,768]{1,0:T(8,128)(2,1)}, bf16[768,256]{1,0:T(8,128)(2,1)})) %all-reduce.11.cloned.1.call-update) | async-done | bytes 2752528 | tf_op jit(solution)/shard_map/psum | solution.py:386
  467.0 8.5 %shard_map.367 = bf16[8,64,64]{2,1,0:T(8,128)(2,1)} custom-call(bf16[8,64,64]{2,1,0:T(8,128)(2,1)} %bitcast.247), custom_call_target="tpu_custom_call" | custom-call | tf_op jit(solution)/shard_map/pallas_call | solution.py:111
  475.5 40.5 %all-reduce.3 = (f32[768]{0:T(1024)}, f32[768]{0:T(1024)}, f32[768]{0:T(1024)}, f32[768]{0:T(1024)}, f32[256]{0:T(256)}) all-reduce(f32[768]{0:T(1024)S(1)} %copy-done.86, f32[768]{0:T(1024)S(1)} %copy-done.87, f32[768]{0:T(1024)S(1)} %copy-done.85, f32[768]{0:T(1024)S(1)} %reduce_sum.302, ...), channel_id=1, replica_groups=mesh['dp'=8,'mp'=4] {'dp'}, use_global_device_ids=true, to_apply=%region_33.34 | all-reduce | flops 3328 | bytes 26624 | tf_op jit(solution)/shard_map/psum | solution.py:481
  516.7 4.5 slice_add_fusion
  521.1 5.0 fusion.1
  526.1 6.3 %convolution_add_fusion = f32[8000,64]{0,1:T(8,128)} fusion(f32[8000,64]{0,1:T(8,128)S(1)} %fusion.1, f32[256,8000]{0,1:T(8,128)} %copy-done.2, f32[256]{0:T(256)S(1)} %get-tuple-element.137, bf16[256,256]{1,0:T(8,128)(2,1)S(1)} %bitcast.228, s32[]{:T(128)S(6)} %select_n.74), kind=kOutput, calls=%fused_computation.13 | convolution fusion | flops 266752000 | bytes 12370948 | tf_op jit(solution)/shard_map/while/body/eval_jaxpr/mr,mc->rc/dot_general | solution.py:27
  536.6 35.5 %all-reduce.9.cloned.1.call-done = (bf16[64,768]{1,0:T(8,128)(2,1)}, bf16[4,768,192]{1,2,0:T(8,128)(2,1)}, bf16[768,192]{0,1:T(8,128)(2,1)}, bf16[768,192]{0,1:T(8,128)(2,1)}, bf16[192,768]{1,0:T(8,128)(2,1)}) async-done(((bf16[64,768]{1,0:T(8,128)(2,1)}, bf16[4,768,192]{1,2,0:T(8,128)(2,1)}, bf16[768,192]{0,1:T(8,128)(2,1)}, bf16[768,192]{0,1:T(8,128)(2,1)}, bf16[192,768]{1,0:T(8,128)(2,1)}), ...) | async-done | bytes 2162704 | tf_op jit(solution)/shard_map/psum | solution.py:480
  (395 shorter events, 163.5 us)
Async XLA Ops:
  7.2 104.0 %copy-start = (bf16[768,768]{1,0:T(8,128)(2,1)S(1)}, bf16[768,768]{1,0:T(8,128)(2,1)}, u32[]{:S(2)}) copy-start(bf16[768,768]{1,0:T(8,128)(2,1)} %param.46) | copy-start | bytes 3538948
  7.2 33.3 %copy-start.117 = (s32[2]{0:T(128)S(1)}, s32[2]{0:T(128)}, u32[]{:S(2)}) copy-start(s32[2]{0:T(128)} %param.32) | copy-start | bytes 28
  7.2 45.7 %copy-start.17 = (bf16[2,512,768]{2,1,0:T(8,128)(2,1)S(1)}, bf16[2,512,768]{2,1,0:T(8,128)(2,1)}, u32[]{:S(2)}) copy-start(bf16[2,512,768]{2,1,0:T(8,128)(2,1)} %param.31) | copy-start | bytes 4718596
  7.2 175.9 %all-gather.2.cloned.1.call-start = ((), (), s32[]{:S(2)}) async-start(), calls=%async_computation | async-start | bytes 5160960 | tf_op jit(solution)/shard_map/all_gather | solution.py:226
  8.0 453.0 %all-reduce.11.cloned.1.call-start = ((), (), s32[]{:S(2)}) async-start(), calls=%async_computation.2 | async-start | bytes 5505024 | tf_op jit(solution)/shard_map/psum | solution.py:386
  9.7 46.1 %copy-start.101 = (s32[256]{0:T(256)}, s32[256]{0:T(256)S(1)}, u32[]{:S(2)}) copy-start(s32[256]{0:T(256)S(1)} %convert_add_fusion.4) | copy-start | bytes 3076
  25.9 29.9 %copy-start.106 = (s32[2,128]{1,0:T(2,128)S(1)}, s32[2,128]{1,0:T(2,128)}, u32[]{:S(2)}) copy-start(s32[2,128]{1,0:T(2,128)} %param.34) | copy-start | bytes 3076
  25.9 29.9 %copy-start.107 = (s32[2,128]{1,0:T(2,128)S(1)}, s32[2,128]{1,0:T(2,128)}, u32[]{:S(2)}) copy-start(s32[2,128]{1,0:T(2,128)} %param.33) | copy-start | bytes 3076
  127.0 30.1 %copy-start.73 = (f32[768]{0:T(1024)S(1)}, f32[768]{0:T(1024)}, u32[]{:S(2)}) copy-start(f32[768]{0:T(1024)} %param.44) | copy-start | bytes 9220
  127.0 30.1 %copy-start.96 = (f32[768]{0:T(1024)S(1)}, f32[768]{0:T(1024)}, u32[]{:S(2)}) copy-start(f32[768]{0:T(1024)} %param.45) | copy-start | bytes 9220
  262.7 30.4 %copy-start.75 = (f32[768]{0:T(1024)S(1)}, f32[768]{0:T(1024)}, u32[]{:S(2)}) copy-start(f32[768]{0:T(1024)} %param.44) | copy-start | bytes 9220
  339.1 233.0 %all-reduce.9.cloned.1.call-start = ((), (), s32[]{:S(2)}) async-start(), calls=%async_computation.1 | async-start | bytes 4325376 | tf_op jit(solution)/shard_map/psum | solution.py:480
  384.4 76.6 %copy-start.100 = (s32[256]{0:T(256)S(1)}, s32[256]{0:T(256)}, u32[]{:S(2)}) copy-start(s32[256]{0:T(256)} %sub.154) | copy-start | bytes 3076
  384.4 76.7 %copy-start.21 = (bf16[1280,768]{1,0:T(8,128)(2,1)S(1)}, bf16[1280,768]{1,0:T(8,128)(2,1)}, u32[]{:S(2)}) copy-start(bf16[1280,768]{1,0:T(8,128)(2,1)} %copy-done.20) | copy-start | bytes 5898244
  385.9 77.3 %copy-start.89 = (s32[8,64]{1,0:T(8,128)S(1)}, s32[8,64]{1,0:T(8,128)}, u32[]{:S(2)}) copy-start(s32[8,64]{1,0:T(8,128)} %get-tuple-element.117) | copy-start | bytes 6148
  385.9 77.4 %copy-start.25 = (bf16[8,32,256]{2,1,0:T(8,128)(2,1)S(1)}, bf16[8,32,256]{2,1,0:T(8,128)(2,1)}, u32[]{:S(2)}) copy-start(bf16[8,32,256]{2,1,0:T(8,128)(2,1)} %shard_map.363) | copy-start | bytes 393220
  461.1 54.9 %copy-start.92 = (f32[256]{0:T(256)S(1)}, f32[256]{0:T(256)}, u32[]{:S(2)}) copy-start(f32[256]{0:T(256)} %copy-done.91) | copy-start | bytes 3076
  461.1 54.9 %copy-start.99 = (f32[256]{0:T(256)S(1)}, f32[256]{0:T(256)}, u32[]{:S(2)}) copy-start(f32[256]{0:T(256)} %get-tuple-element.160) | copy-start | bytes 3076
  461.2 54.9 %copy-start.104 = (f32[256]{0:T(256)S(1)}, f32[256]{0:T(256)}, u32[]{:S(2)}) copy-start(f32[256]{0:T(256)} %copy-done.103) | copy-start | bytes 3076
  461.2 55.5 %copy-start.109 = (s32[2,128]{1,0:T(2,128)S(1)}, s32[2,128]{1,0:T(2,128)}, u32[]{:S(2)}) copy-start(s32[2,128]{1,0:T(2,128)} %copy-done.108) | copy-start | bytes 3076
  461.2 55.5 %copy-start.111 = (s32[2,128]{1,0:T(2,128)S(1)}, s32[2,128]{1,0:T(2,128)}, u32[]{:S(2)}) copy-start(s32[2,128]{1,0:T(2,128)} %copy-done.110) | copy-start | bytes 3076
  461.2 55.5 %copy-start.113 = (f32[2,128]{1,0:T(2,128)S(1)}, f32[2,128]{1,0:T(2,128)}, u32[]{:S(2)}) copy-start(f32[2,128]{1,0:T(2,128)} %copy-done.112) | copy-start | bytes 3076
  475.5 45.6 %copy-start.63 = (bf16[8,64,64]{2,1,0:T(8,128)(2,1)S(1)}, bf16[8,64,64]{2,1,0:T(8,128)(2,1)}, u32[]{:S(2)}) copy-start(bf16[8,64,64]{2,1,0:T(8,128)(2,1)} %shard_map.367) | copy-start | bytes 196612
  534.0 45.2 %copy-start.1 = (bf16[768,768]{1,0:T(8,128)(2,1)S(1)}, bf16[768,768]{1,0:T(8,128)(2,1)}, u32[]{:S(2)}) copy-start(bf16[768,768]{1,0:T(8,128)(2,1)} %param.46) | copy-start | bytes 3538948
  (104 other events, 465.8 us)
Sparse Core Ops, SparseCore 0:
  9.6 37.2 all-gather.1
  339.2 121.7 all-reduce.10
  466.3 105.7 all-reduce.8

commit v2 on v1

--- a/solution.py
+++ b/solution.py
@@ -122,90 +122,685 @@
     )(*values)
 
 
-def sum_kernel(chunks, x_ref, o_ref, r1, s2, r2, send_sems, recv_sems):
-    me = lax.axis_index("mp")
-    b0 = lax.rem(me, 2)
-    b1 = me // 2
-    p1 = me + 1 - 2 * b0
-    p2 = lax.rem(me + 2, 4)
-    half = r1.shape[1]
-    quarter = half // 2
+def contract(first_op, second_op, first_dim, second_dim):
+    return lax.dot_general(
+        first_op, second_op, (((first_dim,), (second_dim,)), ((), ())), preferred_element_type=F32
+    )
+
+
+def span(start, count):
+    return pl.ds(pl.multiple_of(start, 16), count)
+
+
+def each(count, step, body, unroll=1):
+    def run(index, carry):
+        body(pl.multiple_of(index * step, step))
+        return carry
+
+    lax.fori_loop(0, count // step, run, 0, unroll=unroll)
+
+
+def sum8(value):
+    return jnp.sum(value.reshape(value.shape[0] // 8, 8, value.shape[1]), axis=0)
+
+
+class Quarters:
+    def __init__(self, part, r1, s2, r2, full, send, recv):
+        self.part, self.r1, self.s2, self.r2, self.full = part, r1, s2, r2, full
+        self.send, self.recv = send, recv
+        me = lax.axis_index("mp")
+        self.b0, self.b1 = lax.rem(me, 2), me // 2
+        self.p1, self.p2 = me + 1 - 2 * self.b0, lax.rem(me + 2, 4)
+        self.length = part.shape[1]
+        self.half = self.length // 2
+        self.quarter = self.length // 4
+
+    def copy(self, s, k, src, dst, peer):
+        return remote(src, dst, self.send.at[s, k], self.recv.at[s, k], "mp", peer)
+
+    def first(self, s):
+        rows = span((1 - self.b0) * self.half, self.half)
+        return self.copy(s, 0, self.part.at[s, rows], self.r1.at[s], self.p1)
+
+    def second(self, s):
+        return self.copy(s, 1, self.s2.at[s], self.r2.at[s], self.p2)
+
+    def place(self, s, h, q):
+        return self.full.at[span(s * self.length + h * self.half + q * self.quarter, self.quarter)]
+
+    def third(self, s, q):
+        return self.copy(s, 2, self.place(s, self.b0, q), self.place(s, self.b0, q), self.p2)
+
+    def fourth(self, s, h):
+        return self.copy(s, 3, self.place(s, h, self.b1), self.place(s, h, self.b1), self.p1)
+
+    def fifth(self, s, h):
+        q = 1 - self.b1
+        return self.copy(s, 4, self.place(s, h, q), self.place(s, h, q), self.p1)
+
+    def both(self, s, q, row):
+        mine = self.part[s, span(self.b0 * self.half + q * self.quarter + row, 16)]
+        return mine.astype(F32) + self.r1[s, span(q * self.quarter + row, 16)].astype(F32)
+
+    def begin(self, s):
+        self.first(s).start()
+
+    def pass_on(self, s):
+        self.first(s).wait_recv()
+
+        def body(row):
+            self.s2[s, span(row, 16)] = self.both(s, 1 - self.b1, row).astype(BF)
+
+        each(self.quarter, 16, body)
+        self.second(s).start()
+
+    def wait_sum(self, s):
+        self.second(s).wait_recv()
+
+    def total(self, s, row):
+        return self.both(s, self.b1, row) + self.r2[s, span(row, 16)].astype(F32)
+
+    def own_row(self, s, row):
+        return s * self.length + self.b0 * self.half + self.b1 * self.quarter + row
+
+    def spread(self, s):
+        self.third(s, self.b1).start()
+        self.fourth(s, self.b0).start()
+
+    def forward(self, s):
+        self.third(s, 1 - self.b1).wait_recv()
+        self.fifth(s, self.b0).start()
+
+    def wait_full(self, s):
+        self.fourth(s, 1 - self.b0).wait_recv()
+        self.fifth(s, 1 - self.b0).wait_recv()
+
+    def drain(self, s):
+        self.first(s).wait_send()
+        self.second(s).wait_send()
+        self.third(s, self.b1).wait_send()
+        self.fourth(s, self.b0).wait_send()
+        self.fifth(s, self.b0).wait_send()
+
+
+def scaled(center):
+    return lax.rsqrt(jnp.mean(center * center, axis=-1, keepdims=True) + EPSILON)
+
+
+def scores_of(qkv, sT, h, cols, word_length):
+    k_cols = pl.ds(cols.start, word_length), pl.ds(cols.start + word_length, cols.size - word_length)
+    sT[0:word_length] = contract(qkv[h, 128:192, k_cols[0]], qkv[h, 0:64, cols], 0, 0)
+    sT[word_length:] = contract(qkv[h, 128:192, k_cols[1]], qkv[h, 64:128, cols], 0, 0)
+
+
+def forward_kernel(
+    sizes, stream, query_weight, w_key, w_value, mask, w_out, w_up, w_down, norms,
+    qkv, lse, ctx, wt_words, wt_ents, center1, first_low, hidden, slope, center2, out,
+    sT, pT, pre, first, part1, r11, s21, r21, part2, r12, s22, r22,
+    send1, recv1, send2, recv2,
+):
+    seqs, length, word_length, heads = sizes
+    width = stream.shape[1]
+    units = w_up.shape[1]
+    one = Quarters(part1, r11, s21, r21, first_low, send1, recv1)
+    two = Quarters(part2, r12, s22, r22, center2, send2, recv2)
     barrier = pltpu.get_barrier_semaphore()
-    for peer in (p1, p2):
+    for peer in (one.p1, one.p2):
         pl.semaphore_signal(barrier, inc=1, device_id={"mp": peer}, device_id_type=MESH)
+
+    for target, first_query in ((wt_words, 0), (wt_ents, 2)):
+        sources = (query_weight[first_query], query_weight[first_query + 1], w_key[...], w_value[...])
+        for g, source in enumerate(sources):
+            turned = jnp.transpose(source)
+            for h in range(heads):
+                target[h, g * DH : (g + 1) * DH] = turned[h * DH : (h + 1) * DH]
+
+    def project(s):
+        for weight, start, count in ((wt_words, 0, word_length), (wt_ents, word_length, length - word_length)):
+            base = s * length + start
+            for h in range(heads):
+                value = contract(weight[h], stream[base : base + count], 1, 1)
+                qkv[h, 0:128, base : base + count] = (value[0:128] * 0.125).astype(BF)
+                qkv[h, 128:256, base : base + count] = value[128:256].astype(BF)
+
+    def attend(s, h):
+        cols = pl.ds(s * length, length)
+        scores_of(qkv, sT, h, cols, word_length)
+
+        def body(col):
+            here = pl.ds(col, LANES)
+            words = sT[0:word_length, here] + mask[s]
+            ents = sT[word_length:, here]
+            top = jnp.maximum(
+                jnp.max(words, axis=0, keepdims=True), jnp.max(ents, axis=0, keepdims=True)
+            )
+            words = jnp.exp(words - top)
+            ents = jnp.exp(ents - top)
+            total = jnp.sum(words, axis=0, keepdims=True) + jnp.sum(ents, axis=0, keepdims=True)
+            pT[0:word_length, here] = words.astype(BF)
+            pT[word_length:, here] = ents.astype(BF)
+            lse[h, 0:1, pl.ds(pl.multiple_of(s * length + col, LANES), LANES)] = top + jnp.log(total)
+            lse[h, 1:2, pl.ds(pl.multiple_of(s * length + col, LANES), LANES)] = 1.0 / total
+
+        each(length, LANES, body)
+        value = matmul(qkv[h, 192:256, cols], pT[...]) * lse[h, 1:2, cols]
+        ctx[h * DH : (h + 1) * DH, cols] = value.astype(BF)
+
+    def attention_part(s):
+        value = contract(ctx[:, s * length : (s + 1) * length], w_out[...], 0, 0)
+        part1[s] = value.astype(BF)
+
+    def first_rows(s):
+        def body(row):
+            at = one.own_row(s, row)
+            value = stream[span(at, 16)].astype(F32) + one.total(s, row)
+            center = value - jnp.mean(value, axis=-1, keepdims=True)
+            mine = span(s * one.quarter + row, 16)
+            center1[mine] = center
+            normed = center * scaled(center) * norms[0:1] + norms[1:2]
+            first[mine] = normed
+            first_low[span(at, 16)] = normed.astype(BF)
+
+        each(one.quarter, 16, body)
+
+    def second_rows(s):
+        def body(row):
+            at = two.own_row(s, row)
+            value = first[span(s * two.quarter + row, 16)] + two.total(s, row)
+            center = value - jnp.mean(value, axis=-1, keepdims=True)
+            center2[span(at, 16)] = center.astype(BF)
+
+        each(two.quarter, 16, body)
+
+    def feed(s):
+        rows = slice(s * length, (s + 1) * length)
+        tile = 256
+        for j in range(units // tile):
+            cols = slice(j * tile, (j + 1) * tile)
+            pre[...] = matmul(first_low[rows], w_up[:, cols])
+
+            def body(row):
+                value = pre[pl.ds(row, 32)]
+                bell = lax.erf(value * 0.7071067811865476) * 0.5 + 0.5
+                at = span(s * length + row, 32)
+                hidden[at, cols] = (value * bell).astype(BF)
+                slope[at, cols] = (
+                    bell + value * jnp.exp(value * value * -0.5) * 0.3989422804014327
+                ).astype(BF)
+
+            each(length, 32, body)
+        for j in range(width // tile):
+            cols = slice(j * tile, (j + 1) * tile)
+            part2[s, :, cols] = matmul(hidden[rows], w_down[:, cols]).astype(BF)
+
+    def output_rows(s):
+        def body(row):
+            at = span(s * length + row, 16)
+            center = center2[at].astype(F32)
+            out[at] = (center * scaled(center) * norms[2:3] + norms[3:4]).astype(BF)
+
+        each(length, 16, body)
+
+    project(0)
+    for h in range(heads):
+        attend(0, h)
+    attention_part(0)
     pl.semaphore_wait(barrier, 2)
-
-    def rows(c, h, q, count):
-        return pl.ds(pl.multiple_of(c * 2 * half + h * half + q * quarter, 16), count)
-
-    def first(c):
-        return remote(
-            x_ref.at[rows(c, 1 - b0, 0, half)], r1.at[c], send_sems.at[c, 0], recv_sems.at[c, 0],
-            "mp", p1,
+    one.begin(0)
+    project(1)
+    attend(1, 0)
+    one.pass_on(0)
+    for h in range(1, heads):
+        attend(1, h)
+    attention_part(1)
+    one.begin(1)
+    one.wait_sum(0)
+    first_rows(0)
+    one.spread(0)
+    one.pass_on(1)
+    one.forward(0)
+    one.wait_full(0)
+    feed(0)
+    two.begin(0)
+    one.wait_sum(1)
+    first_rows(1)
+    one.spread(1)
+    two.pass_on(0)
+    one.forward(1)
+    one.wait_full(1)
+    feed(1)
+    two.begin(1)
+    two.wait_sum(0)
+    second_rows(0)
+    two.spread(0)
+    two.pass_on(1)
+    two.forward(0)
+    two.wait_full(0)
+    output_rows(0)
+    two.wait_sum(1)
+    second_rows(1)
+    two.spread(1)
+    two.forward(1)
+    two.wait_full(1)
+    output_rows(1)
+    for s in range(seqs):
+        one.drain(s)
+        two.drain(s)
+
+
+def quarter_scratch(seqs, length, width):
+    return [
+        pltpu.VMEM((seqs, length, width), BF),
+        pltpu.VMEM((seqs, length // 2, width), BF),
+        pltpu.VMEM((seqs, length // 4, width), BF),
+        pltpu.VMEM((seqs, length // 4, width), BF),
+    ]
+
+
+def forward_layer(sizes, stream, query_weight, w_key, w_value, mask, w_out, w_up, w_down, norms):
+    seqs, length, word_length, heads = sizes
+    tokens, width = stream.shape
+    local = heads * DH
+    units = w_up.shape[1]
+
+    def like(*shape, dtype=BF):
+        return jax.ShapeDtypeStruct(shape, dtype)
+
+    outs = [
+        like(heads, 4 * DH, tokens), like(heads, 8, tokens, dtype=F32), like(local, tokens),
+        like(heads, 4 * DH, width), like(heads, 4 * DH, width), like(tokens // 4, width, dtype=F32),
+        like(tokens, width), like(tokens, units), like(tokens, units), like(tokens, width),
+        like(tokens, width),
+    ]
+    return pl.pallas_call(
+        functools.partial(forward_kernel, sizes),
+        out_shape=outs,
+        in_specs=[VM] * 9,
+        out_specs=[VM] * len(outs),
+        scratch_shapes=[
+            pltpu.VMEM((length, length), F32),
+            pltpu.VMEM((length, length), BF),
+            pltpu.VMEM((length, 256), F32),
+            pltpu.VMEM((tokens // 4, width), F32),
+            *quarter_scratch(seqs, length, width),
+            *quarter_scratch(seqs, length, width),
+            pltpu.SemaphoreType.DMA((seqs, 5)), pltpu.SemaphoreType.DMA((seqs, 5)),
+            pltpu.SemaphoreType.DMA((seqs, 5)), pltpu.SemaphoreType.DMA((seqs, 5)),
+        ],
+        compiler_params=pltpu.CompilerParams(
+            collective_id=3, has_side_effects=True, vmem_limit_bytes=56 * 2**20
+        ),
+    )(stream, query_weight, w_key, w_value, mask, w_out, w_up, w_down, norms)
+
+
+class Job:
+    def __init__(self, buf, out, arrivals, send, recv, n):
+        self.buf, self.out, self.arrivals, self.send, self.recv = buf, out, arrivals, send, recv
+        self.me = lax.axis_index("dp")
+        self.bits, self.halvings = job_plan(buf.shape[0], n)
+
+    def bit(self, k):
+        return lax.rem(self.me // 2**k, 2)
+
+    def peer(self, k):
+        return self.me + (1 - 2 * self.bit(k)) * 2**k
+
+    def offset(self, k):
+        start = 0
+        for i in range(k):
+            start = start + self.bit(i) * (self.buf.shape[0] >> (i + 1))
+        return start
+
+    def copy(self, index, k, src, dst):
+        return remote(src, dst, self.send.at[index], self.recv.at[index], "dp", self.peer(k))
+
+    def steps(self):
+        rows = self.buf.shape[0]
+        size = rows
+        for k in range(self.bits):
+            keep = self.offset(min(k, self.halvings))
+            away = keep
+            if k < self.halvings:
+                size //= 2
+                away = keep + (1 - self.bit(k)) * size
+                keep = keep + self.bit(k) * size
+            arrived = self.arrivals[k]
+            copy = self.copy(k, k, self.buf.at[span(away, size)], arrived)
+            copy.start()
+            yield
+            copy.wait()
+            last = k == self.bits - 1
+
+            def body(row, keep=keep, arrived=arrived, last=last):
+                at = span(keep + row, 16)
+                value = self.buf[at].astype(F32) + arrived[span(row, 16)].astype(F32)
+                (self.out if last else self.buf)[at] = value.astype(BF)
+
+            each(size, 16, body)
+        for k in reversed(range(self.halvings)):
+            done = self.out.at[span(self.offset(k + 1), size)]
+            copy = self.copy(self.bits + k, k, done, done)
+            copy.start()
+            yield
+            copy.wait()
+            size *= 2
+
+
+def job_plan(rows, n):
+    bits, halvings, size = n.bit_length() - 1, 0, rows
+    while halvings < bits - 1 and (size // 2) % 16 == 0:
+        size, halvings = size // 2, halvings + 1
+    return bits, halvings
+
+
+def job_scratch(rows, width, n):
+    bits, halvings = job_plan(rows, n)
+    return [pltpu.VMEM((rows, width), BF)] + [
+        pltpu.VMEM((rows >> min(k + 1, halvings), width), BF) for k in range(bits)
+    ]
+
+
+def backward_kernel(sizes, n, *refs):
+    seqs, length, word_length, heads = sizes
+    refs = list(refs)
+
+    def take(count):
+        taken = refs[:count]
+        del refs[:count]
+        return taken
+
+    (
+        cot_words, cot_ents, d_head, head_grad, center2, slope, hidden, first_low, center1, ctx, qkv, lse,
+        wt_words, wt_ents, stream, mask, w_out, w_up, w_down, norms,
+    ) = take(20)
+    down_out, up_out, head_out, *per_head_out = take(3 + heads)
+    gw, small = take(2)
+    sums, d_own, d_ffn, d_pre, wide, d_attn, d_first, dctx, sT, dpT, pT, dsT, dcat = take(13)
+    part, r1, s2, r2 = take(4)
+    send1, recv1, send2, recv2, job_send, job_recv = take(6)
+    width = stream.shape[1]
+    units = w_up.shape[1]
+    bits = n.bit_length() - 1
+    jobs = []
+    for index, out in enumerate([down_out, up_out, head_out, *per_head_out]):
+        buf, *arrivals = take(1 + bits)
+        jobs.append(Job(buf, out, arrivals, job_send.at[index], job_recv.at[index], n))
+    down_job, up_job, head_job, *per_head = jobs
+    one = Quarters(part, r1, s2, r2, d_attn, send1, recv1)
+    two = Quarters(part, r1, s2, r2, gw, send2, recv2)
+    barrier = pltpu.get_barrier_semaphore()
+    for peer in (one.p1, one.p2):
+        pl.semaphore_signal(barrier, inc=1, device_id={"mp": peer}, device_id_type=MESH)
+    for k in range(bits):
+        pl.semaphore_signal(
+            barrier, inc=1, device_id={"dp": down_job.peer(k)}, device_id_type=MESH
         )
-
-    def second(c):
-        return remote(s2.at[c], r2.at[c], send_sems.at[c, 1], recv_sems.at[c, 1], "mp", p2)
-
-    def third(c, q):
-        place = o_ref.at[rows(c, b0, q, quarter)]
-        return remote(place, place, send_sems.at[c, 2], recv_sems.at[c, 2], "mp", p2)
-
-    def fourth(c, h):
-        place = o_ref.at[rows(c, h, b1, quarter)]
-        return remote(place, place, send_sems.at[c, 3], recv_sems.at[c, 3], "mp", p1)
-
-    def fifth(c, h):
-        place = o_ref.at[rows(c, h, 1 - b1, quarter)]
-        return remote(place, place, send_sems.at[c, 4], recv_sems.at[c, 4], "mp", p1)
-
-    def part(c, q):
-        mine = x_ref[rows(c, b0, q, quarter)].astype(F32)
-        theirs = r1[c, pl.ds(pl.multiple_of(q * quarter, 16), quarter)].astype(F32)
-        return mine + theirs
-
-    for c in range(chunks):
-        first(c).start()
-    for c in range(chunks):
-        first(c).wait_recv()
-        s2[c] = part(c, 1 - b1).astype(BF)
-        second(c).start()
-    for c in range(chunks):
-        own = part(c, b1)
-        second(c).wait_recv()
-        o_ref[rows(c, b0, b1, quarter)] = (own + r2[c].astype(F32)).astype(BF)
-        third(c, b1).start()
-        fourth(c, b0).start()
-    for c in range(chunks):
-        third(c, 1 - b1).wait_recv()
-        fifth(c, b0).start()
-    for c in range(chunks):
-        fourth(c, 1 - b0).wait_recv()
-        fifth(c, 1 - b0).wait_recv()
-        first(c).wait_send()
-        second(c).wait_send()
-        third(c, b1).wait_send()
-        fourth(c, b0).wait_send()
-        fifth(c, b0).wait_send()
-
-
-def sum_mp(part, collective, chunks=2):
-    total, width = part.shape
-    half = total // chunks // 2
+    active = []
+
+    def launch(job):
+        active.append(job.steps())
+        next(active[-1])
+
+    def advance(rounds=1):
+        for _ in range(rounds):
+            for steps in list(active):
+                if next(steps, 0) == 0:
+                    active.remove(steps)
+
+    sums[...] = jnp.zeros_like(sums)
+
+    def second_back(s):
+        start = one.own_row(0, 0)
+
+        def rows_of(row, cot):
+            at = span(s * length + row, 16)
+            center = center2[at].astype(F32)
+            inv = scaled(center)
+            normed = center * inv
+            sums[0] += cot * normed
+            sums[1] += cot
+            grad = cot * norms[2:3]
+            value = inv * (
+                grad
+                - jnp.mean(grad, axis=-1, keepdims=True)
+                - normed * jnp.mean(grad * normed, axis=-1, keepdims=True)
+            )
+            d_ffn[at] = value.astype(BF)
+
+            @pl.when((row >= start) & (row < start + one.quarter))
+            def keep():
+                d_own[span(s * one.quarter + row - start, 16)] = value
+
+        scored = d_head.shape[1]
+
+        def word_rows(row):
+            rows_of(row, cot_words[s, span(row, 16)].astype(F32))
+
+        def scored_rows(row):
+            rows_of(row + word_length, cot_ents[s, span(row, 16)].astype(F32) + d_head[s, span(row, 16)])
+
+        def other_rows(row):
+            row = row + scored
+            rows_of(row + word_length, cot_ents[s, span(row, 16)].astype(F32))
+
+        each(word_length, 16, word_rows)
+        each(scored, 16, scored_rows)
+        each(length - word_length - scored, 16, other_rows)
+
+    def feed_back(s):
+        rows = slice(s * length, (s + 1) * length)
+        tile = 256
+        for j in range(units // tile):
+            cols = slice(j * tile, (j + 1) * tile)
+            wide[...] = contract(d_ffn[rows], w_down[cols], 1, 1)
+
+            def body(row):
+                at = span(s * length + row, 32)
+                d_pre[at, cols] = (wide[pl.ds(row, 32)] * slope[at, cols].astype(F32)).astype(BF)
+
+            each(length, 32, body)
+        for j in range(width // tile):
+            cols = slice(j * tile, (j + 1) * tile)
+            part[s, :, cols] = contract(d_pre[rows], w_up[cols], 1, 1).astype(BF)
+
+    def first_back(s):
+        def body(row):
+            at = one.own_row(s, row)
+            mine = span(s * one.quarter + row, 16)
+            value = d_own[mine] + one.total(s, row)
+            center = center1[mine]
+            inv = scaled(center)
+            normed = center * inv
+            sums[2] += value * normed
+            sums[3] += value
+            grad = value * norms[0:1]
+            value = inv * (
+                grad
+                - jnp.mean(grad, axis=-1, keepdims=True)
+                - normed * jnp.mean(grad * normed, axis=-1, keepdims=True)
+            )
+            d_first[mine] = value
+            d_attn[span(at, 16)] = value.astype(BF)
+
+        each(one.quarter, 16, body)
+
+    def context_back(s):
+        cols = slice(s * length, (s + 1) * length)
+        dctx[:, cols] = contract(w_out[...], d_attn[cols], 1, 1).astype(BF)
+
+    def attend_back(s, h):
+        cols = pl.ds(s * length, length)
+        w_cols = pl.ds(s * length, word_length)
+        e_cols = pl.ds(s * length + word_length, length - word_length)
+        mine = slice(h * DH, (h + 1) * DH)
+        scores_of(qkv, sT, h, cols, word_length)
+        dpT[...] = contract(qkv[h, 192:256, cols], dctx[mine, cols], 0, 0)
+
+        def body(col):
+            here = pl.ds(col, LANES)
+            at = pl.ds(pl.multiple_of(s * length + col, LANES), LANES)
+            delta = jnp.sum(
+                ctx[mine, at].astype(F32) * dctx[mine, at].astype(F32), axis=0, keepdims=True
+            )
+            log_total = lse[h, 0:1, at]
+            probs = jnp.exp(sT[0:word_length, here] + mask[s] - log_total)
+            pT[0:word_length, here] = probs.astype(BF)
+            dsT[0:word_length, here] = (probs * (dpT[0:word_length, here] - delta)).astype(BF)
+            probs = jnp.exp(sT[word_length:, here] - log_total)
+            pT[word_length:, here] = probs.astype(BF)
+            dsT[word_length:, here] = (probs * (dpT[word_length:, here] - delta)).astype(BF)
+
+        each(length, LANES, body)
+        d_words, d_ents = dsT[0:word_length], dsT[word_length:]
+        dcat[h, 0:64, cols] = (contract(qkv[h, 128:192, w_cols], d_words, 1, 0) * 0.125).astype(BF)
+        dcat[h, 64:128, cols] = (contract(qkv[h, 128:192, e_cols], d_ents, 1, 0) * 0.125).astype(BF)
+        dcat[h, 128:192, w_cols] = contract(qkv[h, 0:64, cols], d_words, 1, 1).astype(BF)
+        dcat[h, 128:192, e_cols] = contract(qkv[h, 64:128, cols], d_ents, 1, 1).astype(BF)
+        dcat[h, 192:256, cols] = contract(dctx[mine, cols], pT[...], 1, 1).astype(BF)
+
+    def head_grads(h):
+        buf = per_head[h].buf
+        from_words, from_ents = None, None
+        for s in range(seqs):
+            middle, start, end = s * length + word_length, s * length, (s + 1) * length
+            words = matmul(dcat[h, :, start:middle], stream[start:middle])
+            ents = matmul(dcat[h, :, middle:end], stream[middle:end])
+            from_words = words if s == 0 else from_words + words
+            from_ents = ents if s == 0 else from_ents + ents
+        buf[0:128] = from_words[0:128].astype(BF)
+        buf[128:256] = (from_words[128:256] + from_ents[128:256]).astype(BF)
+        buf[256:384] = from_ents[0:128].astype(BF)
+        buf[384:448] = matmul(ctx[h * DH : (h + 1) * DH], d_attn[...]).astype(BF)
+
+    def stream_part(s):
+        for start in range(0, length, LANES):
+            weight = wt_words if start < word_length else wt_ents
+            cols = slice(s * length + start, s * length + start + LANES)
+            value = contract(dcat[0, :, cols], weight[0], 0, 0)
+            for h in range(1, heads):
+                value = value + contract(dcat[h, :, cols], weight[h], 0, 0)
+            part[s, start : start + LANES] = value.astype(BF)
+
+    def last_rows(s):
+        def body(row):
+            at = two.own_row(s, row)
+            value = d_first[span(s * two.quarter + row, 16)] + two.total(s, row)
+            gw[span(at, 16)] = value.astype(BF)
+
+        each(two.quarter, 16, body)
+
+    def tile_grads(job, left, right):
+        tile = 256
+        for j in range(left.shape[1] // tile):
+            cols = slice(j * tile, (j + 1) * tile)
+            job.buf[cols] = contract(left[:, cols], right[...], 0, 0).astype(BF)
+
+    head_job.buf[...] = head_grad[...]
+    second_back(0)
+    feed_back(0)
+    pl.semaphore_wait(barrier, 2 + bits)
+    one.begin(0)
+    launch(head_job)
+    second_back(1)
+    one.pass_on(0)
+    feed_back(1)
+    one.begin(1)
+    tile_grads(down_job, hidden, d_ffn)
+    launch(down_job)
+    one.wait_sum(0)
+    first_back(0)
+    one.spread(0)
+    one.pass_on(1)
+    tile_grads(up_job, first_low, d_pre)
+    launch(up_job)
+    one.forward(0)
+    one.wait_sum(1)
+    first_back(1)
+    one.spread(1)
+    advance()
+    one.wait_full(0)
+    context_back(0)
+    attend_back(0, 0)
+    one.forward(1)
+    advance()
+    one.wait_full(1)
+    context_back(1)
+    for s in range(seqs):
+        one.drain(s)
+    attend_back(1, 0)
+    head_grads(0)
+    advance()
+    launch(per_head[0])
+    for h in range(1, heads):
+        attend_back(0, h)
+        advance()
+        attend_back(1, h)
+        if h == heads - 1:
+            for s in range(seqs):
+                stream_part(s)
+                two.begin(s)
+        head_grads(h)
+        advance()
+        launch(per_head[h])
+    two.pass_on(0)
+    two.pass_on(1)
+    advance()
+    two.wait_sum(0)
+    last_rows(0)
+    two.spread(0)
+    two.wait_sum(1)
+    last_rows(1)
+    two.spread(1)
+    advance()
+    two.forward(0)
+    two.forward(1)
+    for row in range(4):
+        small[row : row + 1] = jnp.sum(sums[row], axis=0, keepdims=True)
+    small[4:8] = jnp.zeros_like(small[4:8])
+    advance()
+    for s in range(seqs):
+        two.wait_full(s)
+        two.drain(s)
+    while active:
+        advance()
+
+
+def backward_layer(sizes, n, arrays):
+    seqs, length, word_length, heads = sizes
+    stream, w_up = arrays[14], arrays[17]
+    tokens, width = stream.shape
+    units, local = w_up.shape[1], heads * DH
+    head_width = arrays[3].shape[1]
+    bits = n.bit_length() - 1
+    job_shapes = [(units, width), (width, units), (width, head_width)] + [(7 * DH, width)] * heads
+    outs = [jax.ShapeDtypeStruct(shape, BF) for shape in job_shapes + [(tokens, width)]]
+    outs.append(jax.ShapeDtypeStruct((8, width), F32))
+    scratch = [
+        pltpu.VMEM((4, 16, width), F32), pltpu.VMEM((tokens // 4, width), F32),
+        pltpu.VMEM((tokens, width), BF), pltpu.VMEM((tokens, units), BF),
+        pltpu.VMEM((length, 256), F32), pltpu.VMEM((tokens, width), BF),
+        pltpu.VMEM((tokens // 4, width), F32), pltpu.VMEM((local, tokens), BF),
+        pltpu.VMEM((length, length), F32), pltpu.VMEM((length, length), F32),
+        pltpu.VMEM((length, length), BF), pltpu.VMEM((length, length), BF),
+        pltpu.VMEM((heads, 4 * DH, tokens), BF),
+        *quarter_scratch(seqs, length, width),
+        pltpu.SemaphoreType.DMA((seqs, 5)), pltpu.SemaphoreType.DMA((seqs, 5)),
+        pltpu.SemaphoreType.DMA((seqs, 5)), pltpu.SemaphoreType.DMA((seqs, 5)),
+        pltpu.SemaphoreType.DMA((len(job_shapes), 2 * bits)),
+        pltpu.SemaphoreType.DMA((len(job_shapes), 2 * bits)),
+    ]
+    for rows, columns in job_shapes:
+        scratch += job_scratch(rows, columns, n)
     return pl.pallas_call(
-        functools.partial(sum_kernel, chunks),
-        out_shape=jax.ShapeDtypeStruct((total, width), BF),
-        in_specs=[VM],
-        out_specs=VM,
-        scratch_shapes=[
-            pltpu.VMEM((chunks, half, width), BF),
-            pltpu.VMEM((chunks, half // 2, width), BF),
-            pltpu.VMEM((chunks, half // 2, width), BF),
-            pltpu.SemaphoreType.DMA((chunks, 5)),
-            pltpu.SemaphoreType.DMA((chunks, 5)),
-        ],
-        compiler_params=pltpu.CompilerParams(collective_id=collective, has_side_effects=True),
-    )(part.astype(BF))
+        functools.partial(backward_kernel, sizes, n),
+        out_shape=outs,
+        in_specs=[VM] * len(arrays),
+        out_specs=[VM] * len(outs),
+        scratch_shapes=scratch,
+        compiler_params=pltpu.CompilerParams(
+            collective_id=7, has_side_effects=True, vmem_limit_bytes=60 * 2**20
+        ),
+    )(*arrays)
 
 
 def shards(
@@ -260,48 +855,17 @@
         ent_vectors.reshape(seq_count, ent_len, model_width) + span_total / span_width
     ).astype(BF)
     stream = jnp.concatenate([words, ent_low], axis=1)
-    word_query = contract_product("rpa,gay->grpy", words, query_weight[:2])
-    q_ent = contract_product("sed,kdh->kseh", ent_low, query_weight[2:])
-    to_words = jnp.concatenate([word_query[0], q_ent[0]], axis=1).astype(BF)
-    to_ents = jnp.concatenate([word_query[1], q_ent[1]], axis=1).astype(BF)
-    key_rows = contract_product("snd,dh->snh", stream, w_key).astype(BF)
-    value_rows = contract_product("snd,dh->snh", stream, w_value).astype(BF)
-    head_shape = (seq_count, tokens_len, heads_local, DH)
-    words_heads = to_words.reshape(head_shape)
-    ents_heads = to_ents.reshape(head_shape)
-    keys_heads = key_rows.reshape(head_shape)
-    values_heads = value_rows.reshape(head_shape)
-    key_valid = jnp.concatenate(
-        [positions[None, :] < word_count[:, None], jnp.ones((seq_count, ent_len), dtype=bool)],
-        axis=1,
-    )
-
-    def score_rows():
-        word_part = contract_product("sqhc,skhc->shqk", words_heads, keys_heads[:, :word_length])
-        ent_part = contract_product("sqhc,skhc->shqk", ents_heads, keys_heads[:, word_length:])
-        raw_scores = jnp.concatenate([word_part, ent_part], axis=-1) * 0.125
-        return jnp.where(key_valid[:, None, None, :], raw_scores, MASKED_SCORE)
-
-    scores = score_rows()
-    row_max = jnp.max(scores, axis=-1, keepdims=True)
-    log_total = row_max + jnp.log(jnp.sum(jnp.exp(scores - row_max), axis=-1, keepdims=True))
-    prob_low = jnp.exp(scores - log_total).astype(BF)
-    context = (
-        contract_product("shqk,skhc->sqhc", prob_low, values_heads)
-        .reshape(seq_count * tokens_len, local_width)
-        .astype(BF)
-    )
-    attn_sum = sum_mp(matmul(context, w_out), 3).astype(F32)
-    pre_first = stream.reshape(seq_count * tokens_len, model_width).astype(F32) + attn_sum
-    first_norm, first_back = jax.vjp(normalize, pre_first, gain_attn, bias_attn)
-    first_low = first_norm.astype(BF)
-    pre_act = matmul(first_low, w_up)
-    hidden_f, gelu_back = jax.vjp(gelu_exact, pre_act)
-    hidden = hidden_f.astype(BF)
-    ffn_sum = sum_mp(matmul(hidden, w_down), 4).astype(F32)
-    pre_second = first_norm + ffn_sum
-    output, second_back = jax.vjp(normalize, pre_second, gain_ffn, bias_ffn)
-    out_low = output.astype(BF).reshape(seq_count, tokens_len, model_width)
+    key_valid = positions[None, :] < word_count[:, None]
+    mask = jnp.broadcast_to(
+        jnp.where(key_valid, 0.0, MASKED_SCORE)[..., None], (seq_count, word_length, LANES)
+    )
+    norms = jnp.stack([gain_attn, bias_attn, gain_ffn, bias_ffn])
+    sizes = (seq_count, tokens_len, word_length, heads_local)
+    qkv, lse, ctx, wt_words, wt_ents, center1, first_low, hidden, slope, center2, output = forward_layer(
+        sizes, stream.reshape(seq_count * tokens_len, model_width), query_weight, w_key, w_value,
+        mask, w_out, w_up, w_down, norms,
+    )
+    out_low = output.reshape(seq_count, tokens_len, model_width)
     out_words = out_low[:, :word_length]
     out_ents = out_low[:, word_length:]
     head_in = out_low[:, word_length : word_length + masked_len].reshape(
@@ -372,79 +936,27 @@
     d_head_low = d_head_pre.astype(BF)
     grad_head = contract_product("md,me->de", head_in, d_head_low)
     d_head_in = contract_product("me,de->md", d_head_low, w_head)
-    d_output = jnp.concatenate([cot_words, cot_ents], axis=1).astype(F32)
-    d_output = d_output.at[:, word_length : word_length + masked_len].add(
-        d_head_in.reshape(seq_count, masked_len, model_width)
-    )
-    d_output = d_output.reshape(seq_count * tokens_len, model_width)
-    d_second, grad_gain_ffn, grad_bias_ffn = second_back(d_output)
-    d_ffn = d_second.astype(BF)
-    grad_down = contract_product("tf,td->fd", hidden, d_ffn)
-    d_hidden = contract_product("td,fd->tf", d_ffn, w_down)
-    d_pre_act = gelu_back(d_hidden)[0].astype(BF)
-    grad_up = contract_product("td,tf->df", first_low, d_pre_act)
-    early = lax.psum(
-        (grad_down.astype(BF), grad_up.astype(BF), grad_head.astype(BF)), "dp"
-    )
-    d_first = d_second + sum_mp(contract_product("tf,df->td", d_pre_act, w_up), 7).astype(F32)
-    d_pre_first, grad_gain_attn, grad_bias_attn = first_back(d_first)
-    d_attn = d_pre_first.astype(BF)
-    grad_out = contract_product("th,td->hd", context, d_attn)
-    d_context = contract_product("td,hd->th", d_attn, w_out).astype(BF).reshape(head_shape)
-    prob_rows = jnp.exp(score_rows() - log_total)
-    prob_again = prob_rows.astype(BF)
-    d_probs = contract_product("sqhc,skhc->shqk", d_context, values_heads)
-    d_values = (
-        contract_product("shqk,sqhc->skhc", prob_again, d_context)
-        .astype(BF)
-        .reshape(seq_count, tokens_len, local_width)
-    )
-    d_scores = (
-        prob_rows * (d_probs - jnp.sum(prob_rows * d_probs, axis=-1, keepdims=True))
-    ).astype(BF)
-
-    def bound(form, first_op, second_op):
-        return (
-            (contract_product(form, first_op, second_op) * 0.125)
-            .astype(BF)
-            .reshape(seq_count, -1, local_width)
-        )
-
-    d_score_words, d_score_ents = d_scores[..., :word_length], d_scores[..., word_length:]
-    d_to_words = bound("shqk,skhc->sqhc", d_score_words, keys_heads[:, :word_length])
-    d_to_ents = bound("shqk,skhc->sqhc", d_score_ents, keys_heads[:, word_length:])
-    d_keys = jnp.concatenate(
-        [
-            bound("shqk,sqhc->skhc", d_score_words, words_heads),
-            bound("shqk,sqhc->skhc", d_score_ents, ents_heads),
-        ],
-        axis=1,
-    )
-    grad_query = jnp.stack(
-        [
-            contract_product("yir,yiq->rq", words, d_to_words[:, :word_length]),
-            contract_product("yir,yiq->rq", words, d_to_ents[:, :word_length]),
-            contract_product("sed,seh->dh", ent_low, d_to_words[:, word_length:]),
-            contract_product("sed,seh->dh", ent_low, d_to_ents[:, word_length:]),
-        ]
-    )
-    grad_key = contract_product("snd,snh->dh", stream, d_keys)
-    grad_value = contract_product("snd,snh->dh", stream, d_values)
-    d_stream_word = contract_product(
-        "vcr,er->vce", d_to_words[:, :word_length], query_weight[0]
-    ) + contract_product("vcr,er->vce", d_to_ents[:, :word_length], query_weight[1])
-    d_stream_ent = contract_product(
-        "seh,dh->sed", d_to_words[:, word_length:], query_weight[2]
-    ) + contract_product("seh,dh->sed", d_to_ents[:, word_length:], query_weight[3])
-    d_stream = (
-        jnp.concatenate([d_stream_word, d_stream_ent], axis=1)
-        + contract_product("snh,dh->snd", d_keys, w_key)
-        + contract_product("snh,dh->snd", d_values, w_value)
-    )
-    d_stream_sum = sum_mp(d_stream.reshape(seq_count * tokens_len, model_width), 8).astype(F32)
-    d_total = (d_pre_first + d_stream_sum).reshape(seq_count, tokens_len, model_width)
-    d_ent = d_total[:, word_length:].astype(BF)
-    grad_words = d_total[:, :word_length] + contract_product(
+    *sums, d_total, small = backward_layer(
+        sizes, n_dp,
+        (
+            cot_words, cot_ents, d_head_in.reshape(seq_count, masked_len, model_width),
+            grad_head.astype(BF), center2, slope, hidden, first_low, center1, ctx, qkv, lse, wt_words,
+            wt_ents, stream.reshape(seq_count * tokens_len, model_width), mask, w_out, w_up, w_down,
+            norms,
+        ),
+    )
+    grad_down, grad_up, grad_head, *per_head = (a.astype(F32) for a in sums)
+    per_head = jnp.stack(per_head).reshape(heads_local, 7, DH, model_width)
+
+    def columns_of(which):
+        return per_head[:, which].transpose(2, 0, 1).reshape(model_width, local_width)
+
+    grad_query = jnp.stack([columns_of(0), columns_of(1), columns_of(4), columns_of(5)])
+    grad_key, grad_value = columns_of(2), columns_of(3)
+    grad_out = per_head[:, 6].reshape(local_width, model_width)
+    d_total = d_total.reshape(seq_count, tokens_len, model_width)
+    d_ent = d_total[:, word_length:]
+    grad_words = d_total[:, :word_length].astype(F32) + contract_product(
         "sep,sed->spd", inside.astype(BF), (d_ent.astype(F32) / span_width).astype(BF)
     )
     d_ent_flat = d_ent.reshape(ent_total, model_width)
@@ -468,22 +980,10 @@
     table_grad = table_grad + contract_product(
         "tr,tc->rc", (hit[:, None] == row_index[None, :]).astype(BF), hit_rows
     )
-    late, early = lax.optimization_barrier(
-        (
-            (
-                grad_query.astype(BF), grad_key.astype(BF), grad_value.astype(BF),
-                grad_out.astype(BF), grad_ent_proj.astype(BF),
-            ),
-            early,
-        )
-    )
-    late = lax.psum(late, "dp")
-    small = lax.psum(
-        (grad_gain_attn, grad_bias_attn, grad_gain_ffn, grad_bias_ffn, grad_gain_head), "dp"
-    )
-    grad_down, grad_up, grad_head = (a.astype(F32) for a in early)
-    grad_query, grad_key, grad_value, grad_out, grad_ent_proj = (a.astype(F32) for a in late)
-    grad_gain_attn, grad_bias_attn, grad_gain_ffn, grad_bias_ffn, grad_gain_head = small
+    halves = lax.psum(small[2:4], "mp")
+    grad_gain_ffn, grad_bias_ffn, grad_gain_attn, grad_bias_attn, grad_gain_head, grad_ent_proj = lax.psum(
+        (small[0], small[1], halves[0], halves[1], grad_gain_head, grad_ent_proj), "dp"
+    )
     return (
         out_words, out_ents, loss, grad_words, table_grad, grad_ent_proj, grad_query, grad_key,
         grad_value, grad_out, grad_gain_attn, grad_bias_attn, grad_up, grad_down, grad_gain_ffn,

time: 595 us -> 486 us (0.82)
  Pallas kernels: 181 us -> 326 us
  waiting for transfers between devices: 111 us -> 8.16 us
  matrix products: 119 us -> 29.7 us
  other arithmetic: 73.1 us -> 18.6 us
  local copies, waits for them, and re-layouts: 44.8 us -> 35.2 us
    pallas_call x4 -> x2, Pallas kernels: 120 us -> 263 us  [the longest x1 181 us: backward_layer(): pl.pallas_call(functools.partial(backward_kernel, sizes, n), out_shape=ou...]
    psum x2 -> x1, waiting for transfers between devices: 111 us -> 7.44 us  [shards(): lax.psum((small[0], small[1], halves[0], halves[1], grad_gain_head, grad_...]
    dot_general x40 -> x10, matrix products: 78.9 us -> 20.7 us  [contract_product(): return jnp.einsum(form, first_op, second_op, preferred_element_type=F32)]
    dot_general x7 -> x4, matrix products: 26.8 us -> 9.01 us  [matmul(): return jnp.dot(first_op, second_op, preferred_element_type=F32)]
    reduce_sum x5 -> x2, other arithmetic: 15.6 us -> 0.38 us  [normalize(): return center * inv_scale * gain_vec + shift_vec]
    reduce_sum x5 -> x0, other arithmetic: 14 us -> none  [the longest x4 10.3 us: normalize(): center = source - jnp.mean(source, axis=-1, keepdims=True)]
    sub x1 -> x0, matrix products: 13.7 us -> none  [shards(): d_probs - jnp.sum(prob_rows * d_probs, axis=-1, keepdims=True)]
    convert_element_type x10 -> x3, other arithmetic: 15.7 us -> 4.09 us  [shards(): grad_down, grad_up, grad_head, *per_head = (a.astype(F32) for a in sums)]
  transfers between devices with their start and end apart: 3 -> 2, of which waited for: 2 -> 1; matrix products, arithmetic and copies ran while one was open for 19% -> 9% of each run, Pallas kernels for 23% -> 28%
where the time goes in v2:
time: 486 us; the launch traced here: 476 us
  Pallas kernels  326 us (67%)
  blocking collectives  43.1 us (9%)
  local copies, waits for them, and re-layouts  35.2 us (7%)
  matrix products  29.7 us (6%)
  other arithmetic  18.6 us (4%)
  between operations  15.1 us (3%)
  waiting for transfers between devices  8.16 us (2%)
    pallas_call x1, Pallas kernels, backward_layer(): pl.pallas_call(functools.partial(backward_kernel, sizes, n), out_shape=ou...  181 us
    pallas_call x1, Pallas kernels, forward_layer(): pl.pallas_call(functools.partial(forward_kernel, sizes), out_shape=outs,...  82.1 us
    pallas_call x6, Pallas kernels, exchange(): pl.pallas_call(functools.partial(exchange_kernel, axis, n, kinds), out_sh...  63.1 us
    psum x1, blocking collectives, shards(): lax.psum((small[0], small[1], halves[0], halves[1], grad_gain_head, grad_...  36.9 us
    dot_general x10, matrix products, contract_product(): return jnp.einsum(form, first_op, second_op, preferred_element_type=F32)  20.7 us
    unnamed x64, local copies, waits for them, and re-layouts  10.5 us
  transfers between devices with their start and end apart: 2, of which 1 were waited for; matrix products, arithmetic and copies ran while one was open for 9% of the time, Pallas kernels for 28%

profile of v2, /device:TPU:0, one launch (start us, length us, event | category | flops | bytes accessed | tf_op | source)
XLA Modules:
  0.0 476.1 jit_solution(16486573932964083987)
XLA Ops:
  9.0 2.4 copy.71
  12.6 9.8 %shard_map.358 = s32[8,8,128]{2,1,0:T(8,128)} custom-call(s32[8,8,128]{2,1,0:T(8,128)} %pad.11.refs_0_), custom_call_target="tpu_custom_call" | custom-call | tf_op jit(solution)/shard_map/pallas_call | solution.py:111
  25.1 2.5 copy.75.query_weight
  30.8 8.9 %shard_map.359 = bf16[8,64,64]{2,1,0:T(8,128)(2,1)} custom-call(bf16[8,64,64]{2,1,0:T(8,128)(2,1)} %select_select_fusion.1.refs_0_), custom_call_target="tpu_custom_call" | custom-call | tf_op jit(solution)/shard_map/pallas_call | solution.py:111
  39.7 1.8 convolution_convert_fusion.2.refs_0_
  41.5 11.0 %shard_map.360 = (bf16[4,256,64]{2,1,0:T(8,128)(2,1)}, bf16[4,64,768]{2,1,0:T(8,128)(2,1)}) custom-call(bf16[256,64]{1,0:T(8,128)(2,1)} %convolution_convert_fusion.2.refs_0_, bf16[64,768]{1,0:T(8,128)(2,1)} %refs_1_.2), custom_call_target="tpu_custom_call" | custom-call | tf_op jit(solution)/shard_map/pallas_call | solution.py:111
  57.5 82.1 %shard_map.361 = (bf16[3,256,1280]{2,1,0:T(8,128)(2,1)}, f32[3,8,1280]{2,1,0:T(8,128)}, bf16[192,1280]{1,0:T(8,128)(2,1)}, bf16[3,256,768]{2,1,0:T(8,128)(2,1)},...) custom-call(bf16[1280,768]{1,0:T(8,128)(2,1)} %bitcast.88, ...), custom_call_target="tpu_custom_call" | custom-call | tf_op jit(solution)/shard_map/pallas_call | solution.py:415
  140.5 1.8 slice.134
  142.3 2.7 slice.133
  146.4 9.0 %shard_map.362 = bf16[8,32,256]{2,1,0:T(8,128)(2,1)} custom-call(bf16[32,256]{1,0:T(8,128)(2,1)} %multiply_convert_fusion.refs_0_), custom_call_target="tpu_custom_call" | custom-call | tf_op jit(solution)/shard_map/pallas_call | solution.py:111
  156.4 6.5 %copy.78 = bf16[8000,256]{1,0:T(8,128)(2,1)} copy(bf16[8000,256]{0,1:T(8,128)(2,1)} %all-gather.2.cloned.1.call-done) | data formatting | bytes 8192000 | tf_op jit(solution)/shard_map/all_gather | solution.py:821
  162.9 3.7 gather_fusion.1
  167.4 3.9 fusion.47
  172.5 2.0 copy-done.2
  174.6 6.6 %fusion.4 = f32[256,256]{1,0:T(8,128)} fusion(bf16[8000,256]{0,1:T(8,128)(2,1)} %all-gather.2.cloned.1.call-done, f32[256,8000]{0,1:T(8,128)} %copy-done.2, f32[256]{0:T(256)S(1)} %get-tuple-element.161), kind=kOutput, calls=%fused_computation.10 | convolution fusion | flops 1052672000 | bytes 12551168 | tf_op jit(solution)/shard_map/dot_general | solution.py:23
  181.2 14.1 %shard_map.363 = (f32[8,8,256]{2,1,0:T(8,128)}, f32[8,32,256]{2,1,0:T(8,128)}, bf16[8,32,256]{2,1,0:T(8,128)(2,1)}) custom-call(f32[8,256]{1,0:T(8,128)} %copy-done.16, f32[8,32,256]{2,1,0:T(8,128)} %bitcast.102, bf16[8,32,256]{2,1,0:T(8,128)(2,1)} %get-tuple-element.138.refs_2_), custom_call_target="tpu_custom_call" | custom-call | tf_op jit(solution)/shard_map/pallas_call | solution.py:111
  200.9 180.9 %shard_map.364 = (bf16[768,768]{1,0:T(8,128)(2,1)}, bf16[768,768]{1,0:T(8,128)(2,1)}, bf16[768,256]{1,0:T(8,128)(2,1)}, bf16[448,768]{1,0:T(8,128)(2,1)}, bf16[4...) custom-call(bf16[2,512,768]{2,1,0:T(8,128)(2,1)} %refs_0_.1, ...), custom_call_target="tpu_custom_call" | custom-call | tf_op jit(solution)/shard_map/pallas_call | solution.py:794
  385.8 4.0 convert_add_fusion
  390.4 6.2 %psum.50 = f32[2,768]{1,0:T(2,128)S(1)} all-reduce(f32[2,768]{1,0:T(2,128)S(1)} %slice.124), channel_id=1, replica_groups=mesh['dp'=8,'mp'=4] {'mp'}, use_global_device_ids=true, to_apply=%region_14.15 | all-reduce | flops 1536 | bytes 12288 | tf_op jit(solution)/shard_map/psum | solution.py:983
  397.3 10.3 %shard_map.365 = bf16[8,64,64]{2,1,0:T(8,128)(2,1)} custom-call(bf16[8,64,64]{2,1,0:T(8,128)(2,1)} %bitcast.111), custom_call_target="tpu_custom_call" | custom-call | tf_op jit(solution)/shard_map/pallas_call | solution.py:111
  409.3 5.0 %fusion = f32[8000,64]{0,1:T(8,128)S(1)} fusion(s32[768]{0:T(1024)S(1)} %pad_add_fusion, bf16[256,64]{1,0:T(8,128)(2,1)S(1)} %dynamic-slice_negate_fusion, bf16[512,64]{1,0:T(8,128)(2,1)S(1)} %bitcast.116), kind=kOutput, calls=%fused_computation.3 | convolution fusion | flops 792772608 | bytes 2149376 | tf_op jit(solution)/shard_map/tr,tc->rc/dot_general | solution.py:27
  414.4 2.8 convolution_add_fusion
  421.3 36.9 %all-reduce.2 = (f32[768]{0:T(1024)}, f32[768]{0:T(1024)}, f32[768]{0:T(1024)}, f32[768]{0:T(1024)}, f32[256]{0:T(256)}) all-reduce(f32[768]{0:T(1024)S(1)} %get-tuple-element.127, f32[768]{0:T(1024)S(1)} %get-tuple-element.126, f32[768]{0:T(1024)S(1)} %get-tuple-element.125, ...), channel_id=1, replica_groups=mesh['dp'=8,'mp'=4] {'dp'}, use_global_device_ids=true, to_apply=%region_15.16 | all-reduce | flops 3328 | bytes 26624 | tf_op jit(solution)/shard_map/psum | solution.py:984
  459.8 7.4 %all-reduce.5.cloned.1.call-done = f32[64,768]{1,0:T(8,128)} async-done(((f32[64,768]{1,0:T(8,128)}), f32[64,768]{1,0:T(8,128)}) %all-reduce.5.cloned.1.call-update) | async-done | bytes 196624 | tf_op jit(solution)/shard_map/psum | solution.py:984
  (145 shorter events, 38.7 us)
Async XLA Ops:
  7.2 137.9 %copy-start = (bf16[768,256]{1,0:T(8,128)(2,1)S(1)}, bf16[768,256]{1,0:T(8,128)(2,1)}, u32[]{:S(2)}) copy-start(bf16[768,256]{1,0:T(8,128)(2,1)} %param.48) | copy-start | bytes 1179652
  7.2 4.7 copy-start.18
  7.2 4.7 copy-start.19
  7.2 4.7 copy-start.20
  7.3 4.7 copy-start.21
  7.3 16.0 %copy-start.11 = (bf16[768,192]{0,1:T(8,128)(2,1)S(1)}, bf16[768,192]{0,1:T(8,128)(2,1)}, u32[]{:S(2)}) copy-start(bf16[768,192]{0,1:T(8,128)(2,1)} %param.39) | copy-start | bytes 884740
  7.3 16.9 %copy-start.12 = (bf16[768,192]{0,1:T(8,128)(2,1)S(1)}, bf16[768,192]{0,1:T(8,128)(2,1)}, u32[]{:S(2)}) copy-start(bf16[768,192]{0,1:T(8,128)(2,1)} %param.40) | copy-start | bytes 884740
  7.3 149.1 %all-gather.2.cloned.1.call-start = ((), (), s32[]{:S(2)}) async-start(), calls=%async_computation | async-start | bytes 5160960 | tf_op jit(solution)/shard_map/all_gather | solution.py:821
  8.0 459.2 %all-reduce.5.cloned.1.call-start = ((), (), s32[]{:S(2)}) async-start(), calls=%async_computation.1 | async-start | bytes 393216 | tf_op jit(solution)/shard_map/psum | solution.py:984
  25.1 28.0 %copy-start.26 = (s32[2]{0:T(128)S(1)}, s32[2]{0:T(128)}, u32[]{:S(2)}) copy-start(s32[2]{0:T(128)} %param.30) | copy-start | bytes 28
  25.1 28.0 %copy-start.24 = (s32[2,128]{1,0:T(2,128)S(1)}, s32[2,128]{1,0:T(2,128)}, u32[]{:S(2)}) copy-start(s32[2,128]{1,0:T(2,128)} %param.32) | copy-start | bytes 3076
  25.1 28.0 %copy-start.25 = (s32[2,128]{1,0:T(2,128)S(1)}, s32[2,128]{1,0:T(2,128)}, u32[]{:S(2)}) copy-start(s32[2,128]{1,0:T(2,128)} %param.31) | copy-start | bytes 3076
  29.0 25.6 %copy-start.4 = (bf16[2,512,768]{2,1,0:T(8,128)(2,1)S(1)}, bf16[2,512,768]{2,1,0:T(8,128)(2,1)}, u32[]{:S(2)}) copy-start(bf16[2,512,768]{2,1,0:T(8,128)(2,1)} %param.29) | copy-start | bytes 4718596
  140.5 5.2 %copy-start.17 = (f32[256]{0:T(256)S(1)}, f32[256]{0:T(256)}, u32[]{:S(2)}) copy-start(f32[256]{0:T(256)} %param.49) | copy-start | bytes 3076
  156.4 10.2 %copy-start.3 = (bf16[8,32,256]{2,1,0:T(8,128)(2,1)S(1)}, bf16[8,32,256]{2,1,0:T(8,128)(2,1)}, u32[]{:S(2)}) copy-start(bf16[8,32,256]{2,1,0:T(8,128)(2,1)} %shard_map.362) | copy-start | bytes 393220
  174.5 6.6 %copy-start.16 = (f32[8,256]{1,0:T(8,128)}, f32[8,256]{1,0:T(8,128)S(1)}, u32[]{:S(2)}) copy-start(f32[8,256]{1,0:T(8,128)S(1)} %scatter.14.refs_0_) | copy-start | bytes 24580
  200.9 183.5 %copy-start.15 = (bf16[64,768]{1,0:T(8,128)(2,1)S(1)}, bf16[64,768]{1,0:T(8,128)(2,1)}, u32[]{:S(2)}) copy-start(bf16[64,768]{1,0:T(8,128)(2,1)} %refs_1_.2) | copy-start | bytes 294916
  200.9 184.0 %copy-start.13 = (bf16[256,64]{1,0:T(8,128)(2,1)S(1)}, bf16[256,64]{1,0:T(8,128)(2,1)}, u32[]{:S(2)}) copy-start(bf16[256,64]{1,0:T(8,128)(2,1)} %convolution_convert_fusion.2.refs_0_) | copy-start | bytes 98308
  385.8 21.8 %copy-start.7 = (bf16[448,768]{1,0:T(8,128)(2,1)S(1)}, bf16[448,768]{1,0:T(8,128)(2,1)}, u32[]{:S(2)}) copy-start(bf16[448,768]{1,0:T(8,128)(2,1)} %get-tuple-element.113) | copy-start | bytes 2064388
  385.8 21.8 %copy-start.8 = (bf16[448,768]{1,0:T(8,128)(2,1)S(1)}, bf16[448,768]{1,0:T(8,128)(2,1)}, u32[]{:S(2)}) copy-start(bf16[448,768]{1,0:T(8,128)(2,1)} %get-tuple-element.114) | copy-start | bytes 2064388
  385.8 21.8 %copy-start.9 = (bf16[448,768]{1,0:T(8,128)(2,1)S(1)}, bf16[448,768]{1,0:T(8,128)(2,1)}, u32[]{:S(2)}) copy-start(bf16[448,768]{1,0:T(8,128)(2,1)} %get-tuple-element.115) | copy-start | bytes 2064388
  408.0 6.3 %slice-start = ((s8[8192000]{0:T(1024)(128)(4,1)}), s8[4194304]{0:T(1024)(128)(4,1)S(1)}, s32[]{:S(2)}) async-start(s8[8192000]{0:T(1024)(128)(4,1)} %bitcast.86), calls=%async_computation.2 | async-start | bytes 8388608
  409.3 5.0 %slice-start.1 = ((s8[8192000]{0:T(1024)(128)(4,1)}), s8[3997696]{0:T(1024)(128)(4,1)S(1)}, s32[]{:S(2)}) async-start(s8[8192000]{0:T(1024)(128)(4,1)} %bitcast.86), calls=%async_computation.3 | async-start | bytes 7995392
  458.2 10.6 %copy-start.1 = (bf16[768,256]{1,0:T(8,128)(2,1)S(1)}, bf16[768,256]{1,0:T(8,128)(2,1)}, u32[]{:S(2)}) copy-start(bf16[768,256]{1,0:T(8,128)(2,1)} %param.48) | copy-start | bytes 1179652
  (7 other events, 22.3 us)
Sparse Core Ops, SparseCore 0:
  9.7 36.8 all-gather.1
  396.7 70.5 all-reduce.4
